TPU v7x, 256 devices: a whole 4x4x8 slice. The times are simulated.
256 devices in a mesh: gx: 8 (over z), gy: 4 (over x), gz: 8 (over y, core).
Axes of the slice: x: 4, y: 4, z: 8, core: 2. Of those that a mesh axis runs over, the one named last changes fastest.
Arguments:
- rhs: float32 [128, 512, 512], P('gx', 'gz', 'gy'), may hold values from -6 to 6
- mobility: float32 [128, 512, 512], P('gx', 'gz', 'gy'), may hold values from 0.1 to 1
- labels: int32 [128, 512, 512], P('gx', 'gz', 'gy'), may hold values from 0 to 15
- coarse_inverse: float32 [4096, 4096], P(('gx', 'gy', 'gz'))
Outputs:
- solution_field: float32 [128, 512, 512], P('gx', 'gz', 'gy')
- residual: float32 [128, 512, 512], P('gx', 'gz', 'gy')
All inputs are finite; a program needn't handle non-finite values.
Results may differ from a plain program's by a relative error of at most 0.0003.
Values sent between devices are 32-bit elements; how exact they have to be, the bound alone decides.
A program may use at most 128 MiB of HBM per device.

v0:
```python
import jax
import jax.numpy as jnp
from jax import lax
from jax.sharding import PartitionSpec as P

ITERS = 3


def with_halo(cells, sides, width):
    for axis, dim in sides:
        count = lax.axis_size(axis)
        ends = count - 1
        head = lax.slice_in_dim(cells, 0, width, axis=dim)
        tail = lax.slice_in_dim(cells, cells.shape[dim] - width, cells.shape[dim], axis=dim)
        cells = jnp.concatenate(
            [
                lax.ppermute(tail, axis, [(i, (i + 1) % count) for i in range(ends)]),
                cells,
                lax.ppermute(head, axis, [((i + 1) % count, i) for i in range(ends)]),
            ],
            axis=dim,
        )
    return cells


def apply_operator(padded, field, face_x, face_y, face_z):
    total = face_x[1:] * (field - padded[2:, 1:-1, 1:-1]) + face_x[:-1] * (
        field - padded[:-2, 1:-1, 1:-1]
    )
    total = (
        total
        + face_y[:, 1:] * (field - padded[1:-1, 2:, 1:-1])
        + face_y[:, :-1] * (field - padded[1:-1, :-2, 1:-1])
    )
    total = (
        total
        + face_z[:, :, 1:] * (field - padded[1:-1, 1:-1, 2:])
        + face_z[:, :, :-1] * (field - padded[1:-1, 1:-1, :-2])
    )
    return total


def restrict(field, labels, count):
    parts_list = [
        jnp.sum(jnp.where(labels == label_value, field, 0.0)) for label_value in range(count)
    ]
    return jnp.stack(parts_list)


def extend(values, labels):
    result = jnp.zeros(labels.shape, jnp.float32)
    for label_value in range(values.shape[0]):
        result = jnp.where(labels == label_value, values[label_value], result)
    return result


def field_rim(field):
    return with_halo(field, (("gx", 0), ("gy", 2), ("gz", 1)), 1)


def per_device(rhs, mobility, labels, coarse_inverse):
    count = coarse_inverse.shape[0]
    mob_pad = with_halo(mobility, (("gx", 0), ("gy", 2), ("gz", 1)), 1)
    face_x = 0.5 * (mob_pad[1:, 1:-1, 1:-1] + mob_pad[:-1, 1:-1, 1:-1])
    face_y = 0.5 * (mob_pad[1:-1, 1:, 1:-1] + mob_pad[1:-1, :-1, 1:-1])
    face_z = 0.5 * (mob_pad[1:-1, 1:-1, 1:] + mob_pad[1:-1, 1:-1, :-1])
    diag = (
        face_x[1:]
        + face_x[:-1]
        + face_y[:, 1:]
        + face_y[:, :-1]
        + face_z[:, :, 1:]
        + face_z[:, :, :-1]
    )

    def coarse_solve(field, term, wanted):
        sums = restrict(field, labels, count)
        total = None
        gathered = lax.all_gather(sums, ("gx", "gy", "gz"), axis=0, tiled=True)
        if wanted:
            total = lax.psum(term, ("gx", "gy", "gz"))
        values = jnp.dot(coarse_inverse, gathered, precision=lax.Precision.HIGHEST).reshape(
            -1, count
        )
        return (values, total)

    def direction_rim(field):
        return with_halo(field, (("gx", 0), ("gy", 2), ("gz", 1)), 1)

    values, unused = coarse_solve(rhs, jnp.zeros((), jnp.float32), False)
    solution_field = extend(values[0], labels)
    pad_solution = direction_rim(solution_field)
    residual = rhs - apply_operator(pad_solution, solution_field, face_x, face_y, face_z)
    precond = residual / diag
    pad_precond = field_rim(precond)
    applied = apply_operator(pad_precond, precond, face_x, face_y, face_z)
    values, norm_now = coarse_solve(applied, jnp.sum(residual * precond), True)
    shifted = extend(values[0], labels)
    direction = precond - shifted
    pad_direction = direction_rim(direction)
    for step in range(ITERS):
        image = apply_operator(pad_direction, direction, face_x, face_y, face_z)
        alpha = norm_now / lax.psum(jnp.sum(direction * image), ("gx", "gy", "gz"))
        solution_field = solution_field + alpha * direction
        residual = residual - alpha * image
        if step + 1 < ITERS:
            precond = residual / diag
            pad_precond = field_rim(precond)
            applied = apply_operator(pad_precond, precond, face_x, face_y, face_z)
            values, norm_next = coarse_solve(applied, jnp.sum(residual * precond), True)
            ratio = norm_next / norm_now
            shifted = extend(values[0], labels)
            new_direction = precond + ratio * direction - shifted
            pad_direction = direction_rim(new_direction)
            direction = new_direction
            norm_now = norm_next
    return (solution_field, residual)


def solution(mesh):
    in_specs = (
        P("gx", "gz", "gy"),
        P("gx", "gz", "gy"),
        P("gx", "gz", "gy"),
        P(("gx", "gy", "gz"), None),
    )
    out_specs = (P("gx", "gz", "gy"), P("gx", "gz", "gy"))
    return jax.shard_map(
        per_device, mesh=mesh, in_specs=in_specs, out_specs=out_specs, check_vma=False
    )
```

profile of v0, /device:TPU:1, one launch (start us, length us, event | category | flops | bytes accessed | tf_op | source)
XLA Modules:
  0.0 912.3 jit_solution(6363374467015786381)
XLA Ops:
  0.7 3.8 select_reduce_fusion.48
  4.5 10.1 %stack.220 = f32[16]{0:T(128)S(1)} concatenate(f32[1]{0:T(128)} %bitcast, f32[1]{0:T(128)} %bitcast.1, f32[1]{0:T(128)} %bitcast.2, f32[1]{0:T(128)} %bitcast.3, f32[1]{0:T(128)} %bitcast.4, f32[1]{0:T(128)} %bitcast.5, f32[1]{0:T(128)} %bitcast.6, f32[1]{0:T(128)} %bitcast.7, f32[1]{0:T(128)} %bitcast.8, f32[1]{0:T(128)} %bitcast.9, f32[1]{0:T(128)} %bitcast.10, f32[1]{0:T(128)} %bitcast.11, ...), dimensions={0} | concatenate | bytes 128 | tf_op jit(solution)/shard_map/stack | solution.py:47
  15.0 81.4 %all-reduce = f32[4096]{0:T(1024)S(1)} all-reduce(f32[4096]{0:T(1024)S(1)} %dynamic-update-slice), channel_id=1, replica_groups=mesh['gx'=8,'gy'=4,'gz'=8] {'gx','gy','gz'}, use_global_device_ids=true, to_apply=%add | all-reduce | flops 4096 | bytes 32768
  97.5 10.8 %select_select_fusion = f32[16,64,128]{2,1,0:T(8,128)S(1)} fusion(pred[16,64,128]{2,1,0:T(8,128)(4,1)S(1)} %get-tuple-element.109, pred[16,64,128]{2,1,0:T(8,128)(4,1)S(1)} %get-tuple-element.108, pred[16,64,128]{2,1,0:T(8,128)(4,1)S(1)} %get-tuple-element.107, pred[16,64,128]{2,1,0:T(8,128)(4,1)S(1)} %get-tuple-element.106, ...), kind=kLoop, calls=%fused_computation.333 | loop fusion | flops 2097152 | bytes 2621504 | tf_op jit(solution)/shard_map/jit(_where)/select_n | solution.py:53
  109.8 4.0 collective-permute-start.3
  114.6 2.6 collective-permute-start.1
  124.5 4.0 collective-permute-start.4
  136.2 5.4 collective-permute-start.6
  141.6 2.3 collective-permute-start.7
  149.5 3.6 collective-permute-start.11
  154.8 2.8 multiply_reduce_fusion.5
  158.9 4.9 collective-permute-start.13
  167.4 3.0 collective-permute-start.14
  178.7 3.5 collective-permute-start.16
  182.3 4.8 collective-permute-start.17
  187.7 5.2 select_reduce_fusion.32
  192.9 10.1 %stack.237 = f32[16]{0:T(128)S(1)} concatenate(f32[1]{0:T(128)} %bitcast.34, f32[1]{0:T(128)} %bitcast.35, f32[1]{0:T(128)} %bitcast.36, f32[1]{0:T(128)} %bitcast.37, f32[1]{0:T(128)} %bitcast.38, f32[1]{0:T(128)} %bitcast.39, f32[1]{0:T(128)} %bitcast.40, f32[1]{0:T(128)} %bitcast.41, f32[1]{0:T(128)} %bitcast.42, f32[1]{0:T(128)} %bitcast.43, f32[1]{0:T(128)} %bitcast.44, ...), dimensions={0} | concatenate | bytes 128 | tf_op jit(solution)/shard_map/stack | solution.py:47
  203.3 77.1 %all-reduce.1 = f32[4096]{0:T(1024)S(1)} all-reduce(f32[4096]{0:T(1024)S(1)} %dynamic-update-slice.1), channel_id=1, replica_groups=mesh['gx'=8,'gy'=4,'gz'=8] {'gx','gy','gz'}, use_global_device_ids=true, to_apply=%add.1 | all-reduce | flops 4096 | bytes 32768
  281.6 12.4 %select_subtract_fusion.2 = f32[16,64,128]{2,1,0:T(8,128)S(1)} fusion(f32[16,64,128]{2,1,0:T(8,128)S(1)} %get-tuple-element.91, pred[16,64,128]{2,1,0:T(8,128)(4,1)} %copy-done.74, pred[16,64,128]{2,1,0:T(8,128)(4,1)} %copy-done.71, pred[16,64,128]{2,1,0:T(8,128)(4,1)} %copy-done.68, pred[16,64,128]{2,1,0:T(8,128)(4,1)} %copy-done.65, ...), kind=kLoop, calls=%fused_computation.314 | loop fusion | flops 2228224 | bytes 3145792 | tf_op jit(solution)/shard_map/sub | solution.py:99
  295.2 4.3 collective-permute-start.19
  312.7 4.9 collective-permute-start.22
  320.8 2.4 multiply_reduce_fusion.4
  323.2 78.2 %all-reduce.6 = (f32[]{:T(128)}, f32[]{:T(128)}) all-reduce(f32[]{:T(128)} %get-tuple-element.90, f32[]{:T(128)} %get-tuple-element.88), channel_id=1, replica_groups=mesh['gx'=8,'gy'=4,'gz'=8] {'gx','gy','gz'}, use_global_device_ids=true, to_apply=%region_17.18 | all-reduce | flops 2 | bytes 16 | tf_op jit(solution)/shard_map/psum | solution.py:81
  402.7 3.0 multiply_reduce_fusion.3
  406.9 4.2 collective-permute-start.25
  427.5 5.0 collective-permute-start.28
  435.8 5.2 select_reduce_fusion.16
  441.0 10.3 %stack.254 = f32[16]{0:T(128)S(1)} concatenate(f32[1]{0:T(128)} %bitcast.68, f32[1]{0:T(128)} %bitcast.69, f32[1]{0:T(128)} %bitcast.70, f32[1]{0:T(128)} %bitcast.71, f32[1]{0:T(128)} %bitcast.72, f32[1]{0:T(128)} %bitcast.73, f32[1]{0:T(128)} %bitcast.74, f32[1]{0:T(128)} %bitcast.75, f32[1]{0:T(128)} %bitcast.76, f32[1]{0:T(128)} %bitcast.77, f32[1]{0:T(128)} %bitcast.78, ...), dimensions={0} | concatenate | bytes 128 | tf_op jit(solution)/shard_map/stack | solution.py:47
  451.6 78.1 %all-reduce.5 = (f32[4096]{0:T(1024)S(1)}, f32[]{:T(128)}) all-reduce(f32[4096]{0:T(1024)S(1)} %dynamic-update-slice.2, f32[]{:T(128)} %get-tuple-element.85), channel_id=1, replica_groups=mesh['gx'=8,'gy'=4,'gz'=8] {'gx','gy','gz'}, use_global_device_ids=true, to_apply=%add.2 | all-reduce | flops 4097 | bytes 32776
  532.2 12.5 %select_subtract_fusion.1 = f32[16,64,128]{2,1,0:T(8,128)S(1)} fusion(pred[16,64,128]{2,1,0:T(8,128)(4,1)} %copy-done.74, pred[16,64,128]{2,1,0:T(8,128)(4,1)} %copy-done.71, pred[16,64,128]{2,1,0:T(8,128)(4,1)} %copy-done.68, pred[16,64,128]{2,1,0:T(8,128)(4,1)} %copy-done.65, pred[16,64,128]{2,1,0:T(8,128)(4,1)} %copy-done.62, ...), kind=kLoop, calls=%fused_computation.294 | loop fusion | flops 2490368 | bytes 3670084 | tf_op jit(solution)/shard_map/sub | solution.py:113
  546.0 4.2 collective-permute-start.31
  554.4 2.3 collective-permute-start.32
  566.4 4.9 collective-permute-start.34
  574.5 2.4 multiply_reduce_fusion.2
  576.9 77.7 %psum.45 = f32[]{:T(128)} all-reduce(f32[]{:T(128)} %get-tuple-element.83), channel_id=1, replica_groups=mesh['gx'=8,'gy'=4,'gz'=8] {'gx','gy','gz'}, use_global_device_ids=true, to_apply=%region_55.56 | all-reduce | flops 1 | bytes 8 | tf_op jit(solution)/shard_map/psum | solution.py:103
  655.9 3.0 multiply_reduce_fusion.1
  660.2 4.2 collective-permute-start.37
  680.7 5.0 collective-permute-start.40
  688.9 5.4 select_reduce_fusion
  694.3 10.1 %stack.271 = f32[16]{0:T(128)S(1)} concatenate(f32[1]{0:T(128)} %bitcast.102, f32[1]{0:T(128)} %bitcast.103, f32[1]{0:T(128)} %bitcast.104, f32[1]{0:T(128)} %bitcast.105, f32[1]{0:T(128)} %bitcast.106, f32[1]{0:T(128)} %bitcast.107, f32[1]{0:T(128)} %bitcast.108, f32[1]{0:T(128)} %bitcast.109, f32[1]{0:T(128)} %bitcast.110, f32[1]{0:T(128)} %bitcast.111, f32[1]{0:T(128)} %bitcast.112, ...), dimensions={0} | concatenate | bytes 128 | tf_op jit(solution)/shard_map/stack | solution.py:47
  704.7 78.0 %all-reduce.4 = (f32[4096]{0:T(1024)S(1)}, f32[]{:T(128)}) all-reduce(f32[4096]{0:T(1024)S(1)} %dynamic-update-slice.3, f32[]{:T(128)} %get-tuple-element.80), channel_id=1, replica_groups=mesh['gx'=8,'gy'=4,'gz'=8] {'gx','gy','gz'}, use_global_device_ids=true, to_apply=%add.3 | all-reduce | flops 4097 | bytes 32776
  785.2 12.6 %select_subtract_fusion = f32[16,64,128]{2,1,0:T(8,128)S(1)} fusion(pred[16,64,128]{2,1,0:T(8,128)(4,1)} %copy-done.74, pred[16,64,128]{2,1,0:T(8,128)(4,1)} %copy-done.71, pred[16,64,128]{2,1,0:T(8,128)(4,1)} %copy-done.68, pred[16,64,128]{2,1,0:T(8,128)(4,1)} %copy-done.65, pred[16,64,128]{2,1,0:T(8,128)(4,1)} %copy-done.62, ...), kind=kLoop, calls=%fused_computation.274 | loop fusion | flops 2490368 | bytes 3670084 | tf_op jit(solution)/shard_map/sub | solution.py:113
  799.2 4.1 collective-permute-start.43
  807.5 2.5 collective-permute-start.44
  819.8 4.9 collective-permute-start.46
  827.9 2.4 multiply_reduce_fusion
  830.3 77.6 %psum.47 = f32[]{:T(128)} all-reduce(f32[]{:T(128)} %get-tuple-element.78), channel_id=1, replica_groups=mesh['gx'=8,'gy'=4,'gz'=8] {'gx','gy','gz'}, use_global_device_ids=true, to_apply=%region_75.76 | all-reduce | flops 1 | bytes 8 | tf_op jit(solution)/shard_map/psum | solution.py:103
  909.3 2.8 multiply_subtract_fusion
  (379 shorter events, 138.7 us)
Async XLA Ops:
  108.5 10.0 %collective-permute-start.2 = (f32[1,64,128]{2,1,0:T(8,128)S(1)}, f32[1,64,128]{2,1,0:T(8,128)S(1)}, u32[]{:S(2)}, u32[]{:S(2)}) collective-permute-start(f32[1,64,128]{2,1,0:T(8,128)S(1)} %get-tuple-element.155), channel_id=1, source_target_pairs={{32,0},{64,32},{96,64},{128,96},{160,128},{192,160},{224,192},{33,... | collective-permute-start | bytes 98312 | tf_op jit(solution)/shard_map/ppermute | solution.py:19
  109.8 8.7 collective-permute-start.3
  114.6 7.4 collective-permute-start.1
  117.2 4.9 collective-permute-start
  119.1 24.9 %collective-permute-start.8 = (f32[18,64,1]{1,0,2:T(8,128)S(1)}, f32[18,64,1]{1,0,2:T(8,128)S(1)}, u32[]{:S(2)}, u32[]{:S(2)}) collective-permute-start(f32[18,64,1]{1,0,2:T(8,128)S(1)} %copy.314), channel_id=1, source_target_pairs={{0,8},{8,16},{16,24},{1,9},{9,17},{17,25},{2,10},{10,18},{18,26},{... | collective-permute-start | bytes 13832 | tf_op jit(solution)/shard_map/ppermute | solution.py:17
  120.7 24.4 %collective-permute-start.9 = (f32[18,64,1]{1,0,2:T(8,128)S(1)}, f32[18,64,1]{1,0,2:T(8,128)S(1)}, u32[]{:S(2)}, u32[]{:S(2)}) collective-permute-start(f32[18,64,1]{1,0,2:T(8,128)S(1)} %copy.315), channel_id=1, source_target_pairs={{8,0},{16,8},{24,16},{9,1},{17,9},{25,17},{10,2},{18,10},{26,18},{... | collective-permute-start | bytes 13832 | tf_op jit(solution)/shard_map/ppermute | solution.py:19
  124.5 5.7 collective-permute-start.4
  128.8 4.4 collective-permute-start.5
  136.2 16.9 %collective-permute-start.6 = (f32[18,1,130]{2,0,1:T(8,128)S(1)}, f32[18,1,130]{2,0,1:T(8,128)S(1)}, u32[]{:S(2)}, u32[]{:S(2)}) collective-permute-start(f32[18,1,130]{2,0,1:T(8,128)S(1)} %copy.310), channel_id=1, source_target_pairs={{1,0},{2,1},{3,2},{4,3},{5,4},{6,5},{7,6},{9,8},{10,9},{11,10},{12... | collective-permute-start | bytes 28088 | tf_op jit(solution)/shard_map/ppermute | solution.py:19
  141.6 11.5 %collective-permute-start.7 = (f32[18,1,130]{2,0,1:T(8,128)S(1)}, f32[18,1,130]{2,0,1:T(8,128)S(1)}, u32[]{:S(2)}, u32[]{:S(2)}) collective-permute-start(f32[18,1,130]{2,0,1:T(8,128)S(1)} %copy.312), channel_id=1, source_target_pairs={{0,1},{1,2},{2,3},{3,4},{4,5},{5,6},{6,7},{8,9},{9,10},{10,11},{11... | collective-permute-start | bytes 28088 | tf_op jit(solution)/shard_map/ppermute | solution.py:17
  147.5 6.1 collective-permute-start.10
  149.5 4.5 collective-permute-start.11
  157.6 6.2 collective-permute-start.12
  158.9 5.9 collective-permute-start.13
  167.4 5.6 collective-permute-start.14
  171.7 4.5 collective-permute-start.15
  178.7 8.3 collective-permute-start.16
  182.3 5.2 collective-permute-start.17
  293.9 5.6 collective-permute-start.18
  295.2 5.3 collective-permute-start.19
  303.1 4.1 collective-permute-start.20
  305.9 4.4 collective-permute-start.21
  312.7 7.1 collective-permute-start.22
  317.6 3.1 collective-permute-start.23
  405.7 5.5 collective-permute-start.24
  406.9 5.2 collective-permute-start.25
  415.3 5.5 collective-permute-start.26
  419.5 4.7 collective-permute-start.27
  427.5 7.1 collective-permute-start.28
  432.5 3.1 collective-permute-start.29
  544.7 5.5 collective-permute-start.30
  546.0 5.2 collective-permute-start.31
  554.4 5.5 collective-permute-start.32
  558.6 4.7 collective-permute-start.33
  566.4 6.9 collective-permute-start.34
  571.3 3.1 collective-permute-start.35
  658.9 5.5 collective-permute-start.36
  660.2 5.2 collective-permute-start.37
  668.5 5.5 collective-permute-start.38
  672.7 4.7 collective-permute-start.39
  680.7 6.9 collective-permute-start.40
  685.7 3.1 collective-permute-start.41
  797.9 5.4 collective-permute-start.42
  799.2 5.1 collective-permute-start.43
  807.5 5.8 collective-permute-start.44
  812.0 4.7 collective-permute-start.45
  819.8 7.0 collective-permute-start.46
  824.8 3.1 collective-permute-start.47
  (94 other events, 2369.7 us)
where the time goes:
time: 924 us; the launch traced here: 912 us
  blocking collectives  548 us (59%)
  starting transfers between devices  129 us (14%)
  local copies, waits for them, and re-layouts  101 us (11%)
  other arithmetic  98.3 us (11%)
  waiting for transfers between devices  24.5 us (3%)
  between operations  9.58 us (1%)
    unnamed x4, blocking collectives  315 us
    psum x2, blocking collectives, per_device(): alpha = norm_now / lax.psum(jnp.sum(direction * image), ('gx', 'gy', 'gz'))  155 us
    psum x1, blocking collectives, coarse_solve(): total = lax.psum(term, ('gx', 'gy', 'gz'))  78.2 us
    ppermute x24, starting transfers between devices, with_halo(): lax.ppermute(tail, axis, [(i, (i + 1) % count) for i in range(ends)])  72.5 us
    ppermute x24, starting transfers between devices, with_halo(): lax.ppermute(head, axis, [((i + 1) % count, i) for i in range(ends)])  56.2 us
    another operation x4, local copies, waits for them, and re-layouts, restrict(): return jnp.stack(parts_list)  40.7 us
    sub x2, other arithmetic, per_device(): new_direction = precond + ratio * direction - shifted  25.1 us
    slice x24, local copies, waits for them, and re-layouts, with_halo(): head = lax.slice_in_dim(cells, 0, width, axis=dim)  19.9 us
  transfers between devices with their start and end apart: 48, of which 20 were waited for; matrix products, arithmetic and copies ran while one was open for 4% of the time, Pallas kernels for 0%

commit v1 on v0

v1 whole, which is shorter than its diff:
```python
import functools

import jax
import jax.numpy as jnp
from jax import lax
from jax.experimental import pallas as pl
from jax.experimental.pallas import tpu as pltpu
from jax.sharding import PartitionSpec as P

MESH = pl.DeviceIdType.MESH
F32 = jnp.float32
LOOP = 5
VMEM_BYTES = 64 * 1024 * 1024 - 256 * 1024

Y0, Z0, Z1, MOB, LAB, INV = range(6)


def farthest_first(n):
    return sorted(range(n), key=lambda k: -min(k, n - k))


def kernel(
    nx,
    ny,
    nz,
    rhs_hbm,
    mob_hbm,
    lab_hbm,
    inv_hbm,
    x_hbm,
    p_hbm,
    r_hbm,
    w_hbm,
    step_out,
    mob,
    x0,
    y0,
    z0,
    z1,
    p0,
    p1,
    p2,
    rhs,
    lab,
    inv,
    inv_far,
    fx,
    fy,
    fz,
    dinv,
    rim,
    bits,
    fyb,
    fzp,
    xs,
    rs,
    ws,
    xh,
    ys,
    yh,
    zs,
    zh,
    lxh,
    lys,
    lyh,
    lzs,
    lzh,
    lzf,
    yrim_y,
    yrim_z,
    prim_y,
    prim_z,
    zt,
    lt,
    et,
    ey,
    G1_first,
    G2_first,
    G1,
    G2,
    G1_last,
    G2_last,
    in_sem,
    out_sem,
    hs_sem,
    hr_sem,
    gs_sem,
    gr_sem,
):
    cx = rhs.shape[0]
    gx, gy, gz = lax.axis_index("gx"), lax.axis_index("gy"), lax.axis_index("gz")
    sides = (
        ("gx", gx > 0, gx - 1),
        ("gx", gx < nx - 1, gx + 1),
        ("gz", gz > 0, gz - 1),
        ("gz", gz < nz - 1, gz + 1),
        ("gy", gy > 0, gy - 1),
        ("gy", gy < ny - 1, gy + 1),
    )
    fields = {Y0: y0, Z0: z0, Z1: z1, MOB: mob}

    loads = [
        pltpu.make_async_copy(rhs_hbm, rhs, in_sem.at[0]),
        pltpu.make_async_copy(lab_hbm, lab, in_sem.at[1]),
        pltpu.make_async_copy(mob_hbm, mob.at[pl.ds(1, cx)], in_sem.at[2]),
        pltpu.make_async_copy(inv_hbm, inv, in_sem.at[3]),
    ]
    for load in loads:
        load.start()

    def clear(ref, *index):
        ref[index] = jnp.zeros(ref.shape[len(index) :], ref.dtype)

    for low in range(2):

        @pl.when(gx == (nx - 1 if low else 0))
        def _():
            clear(mob, cx + 1 if low else 0)
            clear(lxh, low)
            for e in (Y0, Z0, Z1):
                clear(xh, e, low)

        @pl.when(gz == (nz - 1 if low else 0))
        def _():
            clear(lyh, low)
            for e in (Y0, Z0, Z1, MOB):
                clear(yh, e, low)

        @pl.when(gy == (ny - 1 if low else 0))
        def _():
            clear(lzh, low)
            for e in (Y0, Z0, Z1, MOB):
                clear(zh, e, low)

    barrier = pltpu.get_barrier_semaphore()
    plane_peers = [
        {"gy": lax.rem(gy + j, ny), "gz": lax.rem(gz + k, nz)}
        for j in farthest_first(ny)
        for k in farthest_first(nz)
        if j or k
    ]
    line_peers = [{"gx": lax.rem(gx + k, nx)} for k in farthest_first(nx) if k]
    phases = ((gy * nz + gz, plane_peers), (gx, line_peers))
    partners = plane_peers + line_peers
    for partner in partners:
        pl.semaphore_signal(barrier, inc=1, device_id=partner, device_id_type=MESH)

    for field in (y0, z0, z1):
        clear(field, 0)
        clear(field, cx + 1)

    lane8 = lax.broadcasted_iota(jnp.int32, (8, 128), 1)
    row8 = lax.broadcasted_iota(jnp.int32, (8, 128), 0)
    lane16 = lax.broadcasted_iota(jnp.int32, (16, 128), 1)
    row16 = lax.broadcasted_iota(jnp.int32, (16, 128), 0)
    pair = ((lane8 + 1) >> 1) & 63
    ends = (lane8 == 0) | (lane8 == 127)
    even = (lane8 & 1) == 0
    zero = jnp.zeros((8, 128), F32)

    def fold(plane):
        tiles = [plane[k : k + 8] for k in range(0, plane.shape[0], 8)]
        while len(tiles) > 1:
            tiles = [a + b for a, b in zip(tiles[::2], tiles[1::2])]
        return tiles[0]

    def halo_copy(e, side):
        axis, _, index = sides[side]
        low, other = side & 1, 1 - (side & 1)
        if e == INV:
            src, dst = inv, inv_far.at[side ^ 1]
        elif e == LAB:
            if axis == "gx":
                src, dst = lab.at[cx - 1 if low else 0], lxh.at[other]
            elif axis == "gz":
                src, dst = lys.at[low], lyh.at[other]
            else:
                src, dst = lzs, lzh.at[other]
        elif axis == "gx":
            src = fields[e].at[cx if low else 1]
            dst = mob.at[0 if low else cx + 1] if e == MOB else xh.at[e, other]
        elif axis == "gz":
            src, dst = ys.at[e, low], yh.at[e, other]
        else:
            src, dst = zs.at[e], zh.at[e, other]
        return pltpu.make_async_remote_copy(
            src_ref=src,
            dst_ref=dst,
            send_sem=hs_sem.at[e, side],
            recv_sem=hr_sem.at[e, side ^ 1],
            device_id={axis: index},
            device_id_type=MESH,
        )

    def halo_landed(e, side):
        low = side & 1
        if e == INV:
            ref = inv_far.at[side]
        elif e == LAB:
            ref = (lxh, lyh, lzh)[side // 2].at[low]
        elif side < 2:
            ref = mob.at[cx + 1 if low else 0] if e == MOB else xh.at[e, low]
        else:
            ref = (yh, zh)[side // 2 - 1].at[e, low]
        return pltpu.make_async_copy(ref, ref, hr_sem.at[e, side])

    def exchange_start(e):
        for side in (0, 1, 4, 5, 2, 3):

            @pl.when(sides[side][1])
            def _():
                halo_copy(e, side).start()

    def exchange_wait(e):
        for side in range(6):

            @pl.when(sides[side][1])
            def _():
                halo_landed(e, side).wait()
                halo_copy(e, side).wait_send()

    def stage_rows(rows, x, plane):
        rows[0, pl.ds(x, 1), :] = plane[0:1]
        rows[1, pl.ds(x, 1), :] = plane[63:64]

    def pack_plane(plane):
        packed = plane[0:8]
        for k in range(1, 8):
            packed = jnp.where(pair == k, pltpu.roll(plane[8 * k : 8 * k + 8], 2 * k, 1), packed)
        return jnp.where(pair < 8, packed, jnp.zeros_like(packed))

    def pack_end(tiles, half):
        total = tiles[8 * half]
        for k in range(1, 8):
            total = total + pltpu.roll(tiles[8 * half + k], 16 * k, 1)
        return total

    def stage_plane(e, x, plane):
        stage_rows(ys.at[e], x, plane)
        zt[x] = pack_plane(plane)

    def stage_end(e):
        for half in range(2):
            zs[e, half] = pack_end(zt, half)

    def far(received, half):
        return jnp.where(
            even, pltpu.roll(received[0, half], 1, 1), pltpu.roll(received[1, half], 127, 1)
        )

    def spread(packed, half):
        et[8 * half] = packed
        for k in range(1, 8):
            et[8 * half + k] = pltpu.roll(packed, 128 - 16 * k, 1)

    def edge_part(x, v):
        return edge_tiles(x)

    def edge_tiles(x):
        tile = et[x]
        tiles = [
            jnp.where(ends, tile if k == 0 else pltpu.roll(tile, 128 - 2 * k, 1), 0.0)
            for k in range(8)
        ]
        first, last = ey[0, pl.ds(x, 1), :], ey[1, pl.ds(x, 1), :]
        tiles[0] = tiles[0] + jnp.where(row8 == 0, first, 0.0)
        tiles[7] = tiles[7] + jnp.where(row8 == 7, last, 0.0)
        return jnp.concatenate(tiles, axis=0)

    def apply_all(field, body, init, outer, make=None):
        def step(x, carry, above_v):
            below, v, rest = carry
            above = fx[x + 1] * (above_v - v)
            flux_y = fy[x] * (pltpu.roll(v, 63, 0) - v)
            flux_z = fz[x] * (pltpu.roll(v, 127, 1) - v)
            out = (
                (below - above)
                + (pltpu.roll(flux_y, 1, 0) - flux_y)
                + (pltpu.roll(flux_z, 1, 1) - flux_z)
                + outer(x, v)
            )
            return above, above_v, body(x, v, out, rest)

        if make is None:

            def make(x):
                return field[x + 1]

        v = make(0)
        carry = (fx[0] * (v - field[0]), v, init)
        carry = lax.fori_loop(
            0, cx - 1, lambda x, c: step(x, c, make(x + 1)), carry, unroll=LOOP
        )
        return step(cx - 1, carry, field[cx + 1])[2]

    def subset_sums(values, bits):
        terms = [values]
        for bit in bits:
            terms = terms + [term * bit for term in terms]
        return [fold(term) for term in terms]

    def label_sums(sums):
        sums = list(sums)
        for i in range(4):
            for value in range(16):
                if not value >> i & 1:
                    sums[value] = sums[value] - sums[value | 1 << i]
        return sums

    def bits_of(labels):
        return [((labels >> i) & 1).astype(F32) for i in range(4)]

    def by_label(labels, values):
        return label_sums(subset_sums(values, bits_of(labels)))

    def restrict_plane(x, plane, sums):
        more = subset_sums(plane, [bits[i, x] for i in range(4)])
        return tuple(total + extra for total, extra in zip(sums, more))

    def restrict_rhs(x, sums):
        planes = bits_of(lab[x])
        for i in range(4):
            bits[i, x] = planes[i]
        return tuple(total + extra for total, extra in zip(sums, subset_sums(rhs[x], planes)))

    no_sums = (zero,) * 16

    def rows_of(tiles):
        for shift in (4, 2, 1):
            low = (row8 & shift) == 0
            half = len(tiles) // 2
            merged = []
            for a, b in zip(tiles[:half], tiles[half:]):
                kept, moved = jnp.where(low, a, b), jnp.where(low, b, a)
                if shift == 4:
                    moved = pltpu.roll(moved, 4, 0)
                else:
                    moved = jnp.where(
                        low, pltpu.roll(moved, 8 - shift, 0), pltpu.roll(moved, shift, 0)
                    )
                merged.append(kept + moved)
            tiles = merged
        return tiles[0]

    def placed(sums, block):
        rows = jnp.concatenate([rows_of(list(sums[:8])), rows_of(list(sums[8:]))], axis=0)
        column = jnp.sum(rows, axis=1, keepdims=True)
        return fold(jnp.where(lane16 == 16 * block + row16, column, 0.0))

    def make_tile(sums, parts, dots):
        tiles = [placed(sums, gz) + placed(parts[2], gz - 1) + placed(parts[3], gz + 1)]
        for side in (4, 5, 0, 1):
            tiles.append(placed(parts[side], gz))
        narrow = []
        for dot in dots:
            dot = dot + pltpu.roll(dot, 64, 1)
            narrow.append(dot + pltpu.roll(dot, 32, 1))
        joined = zero
        for k, dot in enumerate(narrow):
            joined = jnp.where(lane8 >> 5 == k, dot, joined)
        return rows_of(tiles + [joined, zero, zero])[:6]

    def neighbour_parts(e, field):
        parts = [
            by_label(lxh[0], -(fx[0] * field[1])),
            by_label(lxh[1], -(fx[cx] * field[cx])),
        ]
        for low in range(2):
            parts.append(by_label(lyh[low], -(fyb[low] * ys[e, low])))
        for keep in (even, ~even):
            halves = [
                by_label(lzf[half], jnp.where(keep, -(fzp[half] * zs[e, half]), 0.0))
                for half in range(2)
            ]
            parts.append([a + b for a, b in zip(*halves)])
        return parts

    def coarse_right_side(e, field):
        sums = apply_all(
            field, lambda x, v, out, s: restrict_plane(x, out, s), no_sums, lambda x, v: rim[x] * v
        )
        return label_sums(sums), neighbour_parts(e, field)

    def slots_of(g, ph):
        if g == 0:
            return (G1_first, G2_first)[ph]
        if g == 4:
            return (G1_last, G2_last)[ph]
        return (G1, G2)[ph].at[g - 1]

    def phase_start(g, ph):
        me, peers = phases[ph]
        slot = slots_of(g, ph).at[me]
        for peer in peers:
            pltpu.make_async_remote_copy(
                src_ref=slot,
                dst_ref=slot,
                send_sem=gs_sem.at[g, ph],
                recv_sem=gr_sem.at[g, ph],
                device_id=peer,
                device_id_type=MESH,
            ).start()

    def phase_wait(g, ph):
        part = slots_of(g, ph).at[pl.ds(0, len(phases[ph][1]))]
        pltpu.make_async_copy(part, part, gr_sem.at[g, ph]).wait()
        pltpu.make_async_copy(part, part, gs_sem.at[g, ph]).wait()

    def shift_down(rows):
        return jnp.concatenate([jnp.zeros((1, 128), F32), rows[: ny - 1]], axis=0)

    def shift_up(rows):
        return jnp.concatenate([rows[1:], jnp.zeros((1, 128), F32)], axis=0)

    def line_sums(slots):
        return [jnp.sum(slots[j * nz : (j + 1) * nz], axis=0) for j in range(ny)]

    def gather(g, tile):
        G1[g - 1, gy * nz + gz] = tile
        phase_start(g, 0)
        phase_wait(g, 0)
        lines = line_sums(G1[g - 1])

        def pick(row):
            return jnp.concatenate([line[row : row + 1] for line in lines], axis=0)

        G2[g - 1, gx, 0:ny] = pick(0) + shift_down(pick(2)) + shift_up(pick(1))
        G2[g - 1, gx, ny : 2 * ny] = pick(3)
        G2[g - 1, gx, 2 * ny : 3 * ny] = pick(4)
        G2[g - 1, gx, 3 * ny : 3 * ny + 1] = sum(lines[1:], lines[0])[5:6]
        phase_start(g, 1)
        phase_wait(g, 1)

    def dots_of(g):
        row = jnp.sum(G2[g - 1, :, 3 * ny : 3 * ny + 1], axis=0)
        lane = lax.broadcasted_iota(jnp.int32, (1, 128), 1)
        return [
            jnp.broadcast_to(
                jnp.sum(jnp.where(lane >> 5 == k, row, 0.0), axis=1, keepdims=True), (1, 128)
            )
            for k in range(3)
        ]

    def right_side(g):
        if g == 0:
            return [G2_first[i] for i in range(nx)]
        blocks = []
        for i in range(nx):
            rows = G2[g - 1, i, 0:ny]
            if i + 1 < nx:
                rows = rows + G2[g - 1, i + 1, ny : 2 * ny]
            if i > 0:
                rows = rows + G2[g - 1, i - 1, 2 * ny : 3 * ny]
            blocks.append(rows)
        return blocks

    def coarse(g):
        accs = [jnp.zeros((16, 128), F32) for _ in range(7)]
        for i, rows in enumerate(right_side(g)):
            for j in range(ny):
                columns = slice((i * ny + j) * 128, (i * ny + j + 1) * 128)
                row = rows[j : j + 1]
                accs[6] = accs[6] + inv[:, columns] * row
                for side in range(6):
                    accs[side] = accs[side] + inv_far[side, :, columns] * row
        lines = []
        for side in range(7):
            total = jnp.sum(accs[side], axis=1, keepdims=True)
            line = jnp.sum(jnp.where(lane16 == row16, total, 0.0), axis=0, keepdims=True)
            if side < 6:
                index = lax.broadcasted_iota(jnp.int32, (1, 128), 1) * 0 + (gx, gz, gy)[side // 2]
                edge = (0, (nx, nz, ny)[side // 2] - 1)[side & 1]
                line = jnp.where(index == edge, 0.0, line)
            lines.append(line)
        return lines

    def take(line, labels):
        return jnp.take_along_axis(
            jnp.broadcast_to(line, labels.shape), labels, axis=1, mode="promise_in_bounds"
        )

    def rim_of(lines):
        x_far = [take(lines[low], lxh[low]) for low in range(2)]
        y_own = [take(lines[6], lys[low]) for low in range(2)]
        y_far = [take(lines[2 + low], lyh[low]) for low in range(2)]
        z_own = [take(lines[6], lzs[half]) for half in range(2)]
        z_far = [
            jnp.where(even, take(lines[4], lzf[half]), take(lines[5], lzf[half]))
            for half in range(2)
        ]
        return x_far, y_own, y_far, z_own, z_far

    def outer_faces(y_own, y_far, z_own, z_far):
        for low in range(2):
            ey[low] = fyb[low] * (y_own[low] - y_far[low])
        for half in range(2):
            spread(fzp[half] * (z_own[half] - z_far[half]), half)

    loads[0].wait()
    loads[1].wait()
    sums = lax.fori_loop(0, cx, restrict_rhs, no_sums, unroll=4)
    line = jnp.sum(placed(label_sums(sums), gz), axis=0, keepdims=True)
    pl.semaphore_wait(barrier, len(partners))
    G1_first[gy * nz + gz] = line
    phase_start(0, 0)
    loads[2].wait()

    def stage_static(x, carry):
        stage_plane(MOB, x, mob[x + 1])
        labels = lab[x]
        stage_rows(lys, x, labels)
        lt[x] = pack_plane(labels)
        return carry

    lax.fori_loop(0, cx, stage_static, 0, unroll=4)
    stage_end(MOB)
    for half in range(2):
        lzs[half] = pack_end(lt, half)
    exchange_start(MOB)
    exchange_start(LAB)
    loads[3].wait()
    exchange_start(INV)

    def faces():
        exchange_wait(MOB)
        exchange_wait(LAB)
        for half in range(2):
            lzf[half] = far(lzh, half)
            fzp[half] = 0.5 * (zs[MOB, half] + far(zh.at[MOB], half))
            spread(fzp[half], half)
        for low in range(2):
            fyb[low] = 0.5 * (ys[MOB, low] + yh[MOB, low])
            ey[low] = fyb[low]
        fx[0] = 0.5 * (mob[1] + mob[0])
        row = lax.broadcasted_iota(jnp.int32, (64, 128), 0)
        lane = lax.broadcasted_iota(jnp.int32, (64, 128), 1)

        def step(x, below):
            m = mob[x + 1]
            above = 0.5 * (mob[x + 2] + m)
            face_y = jnp.where(row == 63, 0.0, 0.5 * (pltpu.roll(m, 63, 0) + m))
            face_z = jnp.where(lane == 127, 0.0, 0.5 * (pltpu.roll(m, 127, 1) + m))
            edges = edge_tiles(x)
            diag = (
                (below + above)
                + (pltpu.roll(face_y, 1, 0) + face_y)
                + (pltpu.roll(face_z, 1, 1) + face_z)
                + edges
            )
            rim[x] = edges
            fx[x + 1] = above
            fy[x] = face_y
            fz[x] = face_z
            dinv[x] = 1.0 / diag
            return above

        lax.fori_loop(0, cx, step, fx[0], unroll=4)

    phase_wait(0, 0)
    for j, row in enumerate(line_sums(G1_first)):
        G2_first[gx, j : j + 1] = row
    phase_start(0, 1)
    faces()
    phase_wait(0, 1)

    exchange_wait(INV)
    lines = coarse(0)

    def first_iterate(x):
        plane = take(lines[6], lab[x])
        x0[x + 1] = plane
        return plane

    x_far, *rest = rim_of(lines)
    x0[0] = x_far[0]
    x0[cx + 1] = x_far[1]
    outer_faces(*rest)

    def first_residual(x, v, out, dot):
        residual = rhs[x] - out
        precond = residual * dinv[x]
        rs[x] = residual
        y0[x + 1] = precond
        stage_plane(Y0, x, precond)
        return dot + fold(residual * precond)

    ry_part = apply_all(x0, first_residual, zero, edge_part, first_iterate)
    stage_end(Y0)
    exchange_start(Y0)
    sums, parts = coarse_right_side(Y0, y0)
    gather(1, make_tile(sums, parts, (ry_part,)))
    lines = coarse(1)
    ry = dots_of(1)[0]

    def first_direction(x):
        plane = y0[x + 1] - take(line_here, lab[x])
        p0[x + 1] = plane
        return plane

    line_here = lines[6]
    direction = first_direction
    exchange_wait(Y0)
    x_far, y_own, y_far, z_own, z_far = rim_of(lines)
    for low in range(2):
        p0[cx + 1 if low else 0] = xh[Y0, low] - x_far[low]
        yrim_y[low] = ys[Y0, low]
        yrim_y[2 + low] = yh[Y0, low]
        yrim_z[low] = zs[Y0, low]
        yrim_z[2 + low] = far(zh.at[Y0], low)
    for k, (y_part, z_part) in enumerate(zip(y_own + y_far, z_own + z_far)):
        prim_y[k] = yrim_y[k] - y_part
        prim_z[k] = yrim_z[k] - z_part

    def prim_faces():
        outer_faces(
            [prim_y[0], prim_y[1]],
            [prim_y[2], prim_y[3]],
            [prim_z[0], prim_z[1]],
            [prim_z[2], prim_z[3]],
        )

    prim_faces()

    alphas = []
    for g, here, scaled, e, after in ((2, p0, z0, Z0, p1), (3, p1, z1, Z1, p2)):

        def image(x, v, out, dots):
            z = out * dinv[x]
            ws[x] = out
            scaled[x + 1] = z
            stage_plane(e, x, z)
            return (
                dots[0] + fold(v * out),
                dots[1] + fold(rs[x] * z),
                dots[2] + fold(out * z),
            )

        dots = apply_all(here, image, (zero, zero, zero), edge_part, direction)
        stage_end(e)
        exchange_start(e)
        sums, parts = coarse_right_side(e, scaled)
        gather(g, make_tile(sums, parts, dots))
        more = coarse(g)
        pw, rz, wz = dots_of(g)
        alpha = ry / pw
        alphas.append(alpha)
        ry_next = ry + alpha * (alpha * wz - 2.0 * rz)
        beta = ry_next / ry
        ry = ry_next
        lines = [line - alpha * extra for line, extra in zip(lines, more)]

        def next_direction(x, here=here, after=after, alpha=alpha, beta=beta, line=lines[6]):
            p = here[x + 1]
            residual = rs[x] - alpha * ws[x]
            rs[x] = residual
            plane = (residual * dinv[x] + beta * p) - take(line, lab[x])
            after[x + 1] = plane
            return plane

        direction = next_direction
        exchange_wait(e)
        x_far, y_own, y_far, z_own, z_far = rim_of(lines)
        for low in range(2):
            outer = cx + 1 if low else 0
            layer = xh[Y0, low] - alpha * xh[e, low]
            xh[Y0, low] = layer
            after[outer] = (layer + beta * here[outer]) - x_far[low]
        z_rows = [ys[e, 0], ys[e, 1], yh[e, 0], yh[e, 1]]
        z_packs = [zs[e, 0], zs[e, 1], far(zh.at[e], 0), far(zh.at[e], 1)]
        for k, (y_part, z_part) in enumerate(zip(y_own + y_far, z_own + z_far)):
            rows = yrim_y[k] - alpha * z_rows[k]
            packs = yrim_z[k] - alpha * z_packs[k]
            yrim_y[k] = rows
            yrim_z[k] = packs
            prim_y[k] = (rows + beta * prim_y[k]) - y_part
            prim_z[k] = (packs + beta * prim_z[k]) - z_part
        prim_faces()

    stores = [
        pltpu.make_async_copy(xs, x_hbm, out_sem.at[0]),
        pltpu.make_async_copy(p2.at[pl.ds(1, cx)], p_hbm, out_sem.at[1]),
        pltpu.make_async_copy(rs, r_hbm, out_sem.at[2]),
        pltpu.make_async_copy(ws, w_hbm, out_sem.at[3]),
    ]

    def last_image(x, v, out, dot):
        ws[x] = out
        return dot + fold(v * out)

    part = apply_all(p2, last_image, zero, edge_part, direction)
    last_tile = jnp.sum(part, axis=0, keepdims=True)
    G1_last[gy * nz + gz] = last_tile
    phase_start(4, 0)
    for store in stores[1:]:
        store.start()

    def join_iterate(x, carry):
        xs[x] = (x0[x + 1] + alphas[0] * p0[x + 1]) + alphas[1] * p1[x + 1]
        return carry

    lax.fori_loop(0, cx, join_iterate, 0, unroll=4)
    stores[0].start()
    phase_wait(4, 0)
    G2_last[gx] = jnp.sum(G1_last[...], axis=0)
    phase_start(4, 1)
    phase_wait(4, 1)
    total = jnp.sum(jnp.sum(G2_last[...], axis=0), axis=1, keepdims=True)
    step_out[...] = jnp.broadcast_to(ry / total, step_out.shape)
    for store in stores:
        store.wait()


def solution(mesh):
    nx, ny, nz = mesh.shape["gx"], mesh.shape["gy"], mesh.shape["gz"]

    def per_device(rhs, mobility, labels, coarse_inverse):
        cx, cy, cz = rhs.shape
        hbm = pl.BlockSpec(memory_space=pl.ANY)

        def vmem(*shape, dtype=F32):
            return pltpu.VMEM(shape, dtype)

        i32 = jnp.int32
        xs, p, rs, w, alpha = pl.pallas_call(
            functools.partial(kernel, nx, ny, nz),
            out_shape=[jax.ShapeDtypeStruct(rhs.shape, F32)] * 4
            + [jax.ShapeDtypeStruct((cy, cz), F32)],
            in_specs=[hbm] * 4,
            out_specs=[hbm] * 4 + [pl.BlockSpec(memory_space=pltpu.VMEM)],
            scratch_shapes=[
                *[vmem(cx + 2, cy, cz) for _ in range(8)],
                vmem(cx, cy, cz),
                vmem(cx, cy, cz, dtype=i32),
                vmem(*coarse_inverse.shape),
                vmem(6, *coarse_inverse.shape),
                vmem(cx + 1, cy, cz),
                *[vmem(cx, cy, cz) for _ in range(4)],
                vmem(4, cx, cy, cz),
                vmem(2, cx, cz),
                vmem(2, 8, 128),
                *[vmem(cx, cy, cz) for _ in range(3)],
                vmem(3, 2, cy, cz),
                vmem(4, 2, cx, cz),
                vmem(4, 2, cx, cz),
                vmem(4, 2, 8, 128),
                vmem(4, 2, 2, 8, 128),
                vmem(2, cy, cz, dtype=i32),
                vmem(2, cx, cz, dtype=i32),
                vmem(2, cx, cz, dtype=i32),
                vmem(2, 8, 128, dtype=i32),
                vmem(2, 2, 8, 128, dtype=i32),
                vmem(2, 8, 128, dtype=i32),
                vmem(4, cx, cz),
                vmem(4, 8, 128),
                vmem(4, cx, cz),
                vmem(4, 8, 128),
                vmem(cx, 8, 128),
                vmem(cx, 8, 128, dtype=i32),
                vmem(cx, 8, 128),
                vmem(2, cx, cz),
                vmem(ny * nz, 1, 128),
                vmem(nx, ny, 128),
                vmem(3, ny * nz, 6, 128),
                vmem(3, nx, 3 * ny + 1, 128),
                vmem(ny * nz, 1, 128),
                vmem(nx, 1, 128),
                pltpu.SemaphoreType.DMA((4,)),
                pltpu.SemaphoreType.DMA((4,)),
                pltpu.SemaphoreType.DMA((6, 6)),
                pltpu.SemaphoreType.DMA((6, 6)),
                pltpu.SemaphoreType.DMA((5, 2)),
                pltpu.SemaphoreType.DMA((5, 2)),
            ],
            compiler_params=pltpu.CompilerParams(
                collective_id=0, has_side_effects=True, vmem_limit_bytes=VMEM_BYTES
            ),
            name="deflated_cg",
        )(rhs, mobility, labels, coarse_inverse)
        return xs + alpha * p, rs - alpha * w

    spec = P("gx", "gz", "gy")
    return jax.shard_map(
        per_device,
        mesh=mesh,
        in_specs=(spec, spec, spec, P(("gx", "gy", "gz"), None)),
        out_specs=(spec, spec),
        check_vma=False,
    )
```

time: 924 us -> 76.8 us (0.08); the launches traced: 912 us -> 76.7 us
  blocking collectives: 548 us -> 0 us
  starting transfers between devices: 129 us -> 0 us
  local copies, waits for them, and re-layouts: 101 us -> 0 us
  other arithmetic: 98.3 us -> 2.72 us
  Pallas kernels: 0 us -> 73.3 us
  waiting for transfers between devices: 24.5 us -> 0 us
    unnamed x4 -> x0, blocking collectives: 315 us -> none
    psum x3 -> x0, blocking collectives: 234 us -> none  [the longest x2 155 us: per_device(): alpha = norm_now / lax.psum(jnp.sum(direction * image), ('gx', 'gy', 'gz'))]
    ppermute x48 -> x0, starting transfers between devices: 129 us -> none  [the longest x24 72.5 us: with_halo(): lax.ppermute(tail, axis, [(i, (i + 1) % count) for i in range(ends)])]
    pallas_call x0 -> x1, Pallas kernels: none -> 73.3 us  [per_device(): pl.pallas_call(functools.partial(kernel, nx, ny, nz), out_shape=[jax.Shap...]
    another operation x4 -> x0, local copies, waits for them, and re-layouts: 40.7 us -> none  [restrict(): return jnp.stack(parts_list)]
    sub x4 -> x1, other arithmetic: 40.3 us -> 2.72 us  [per_device(): return (xs + alpha * p, rs - alpha * w)]
    reduce_sum x10 -> x0, other arithmetic: 35.5 us -> none  [the longest x4 19.6 us: restrict(): jnp.sum(jnp.where(labels == label_value, field, 0.0))]
    slice x50 -> x0, local copies, waits for them, and re-layouts: 31.3 us -> none  [the longest x24 19.9 us: with_halo(): head = lax.slice_in_dim(cells, 0, width, axis=dim)]
  transfers between devices with their start and end apart: 48 -> 0, of which waited for: 20 -> 0; matrix products, arithmetic and copies ran while one was open for 4% -> 0% of each run, Pallas kernels for 0% -> 0%
where the time goes in v1:
time: 76.8 us; the launch traced here: 76.7 us
  Pallas kernels  73.3 us (95%)
  other arithmetic  2.72 us (4%)
    pallas_call x1, Pallas kernels, per_device(): pl.pallas_call(functools.partial(kernel, nx, ny, nz), out_shape=[jax.Shap...  73.3 us
    sub x1, other arithmetic, per_device(): return (xs + alpha * p, rs - alpha * w)  2.72 us

profile of v1, /device:TPU:1, one launch (start us, length us, event | category | flops | bytes accessed | tf_op | source)
XLA Modules:
  0.0 76.7 jit_solution(2166789224272001538)
XLA Ops:
  0.6 73.3 %deflated_cg.1 = (f32[16,64,128]{2,1,0:T(8,128)}, f32[16,64,128]{2,1,0:T(8,128)}, f32[16,64,128]{2,1,0:T(8,128)}, f32[16,64,128]{2,1,0:T(8,128)}, f32[64,128]{1,0:T(8,128)}) custom-call(f32[16,64,128]{2,1,0:T(8,128)} %rhs_hbm.1, f32[16,64,128]{2,1,0:T(8,128)} %mob_hbm.1, s32[16,64,128]{2,1,0:T(8,128)} %lab_hbm.1, f32[16,4096]{1,0:T(8,128)} %inv_hbm.1), custom_call_target="tpu_custom_call" | custom-call | tf_op jit(solution)/shard_map/deflated_cg/pallas_call | solution.py:724
  73.9 2.7 %multiply_subtract_fusion = (f32[16,64,128]{2,1,0:T(8,128)}, f32[16,64,128]{2,1,0:T(8,128)}) fusion(f32[16,64,128]{2,1,0:T(8,128)} %get-tuple-element.10, f32[16,64,128]{2,1,0:T(8,128)} %get-tuple-element.11, f32[64,128]{1,0:T(8,128)} %get-tuple-element.8, f32[16,64,128]{2,1,0:T(8,128)} %get-tuple-element.7, f32[16,64,128]{2,1,0:T(8,128)} %get-tuple-element.9), kind=kLoop, calls=%fused_computation | loop fusion | flops 524288 | bytes 3178496 | tf_op jit(solution)/shard_map/sub | solution.py:779

commit v2 on v1

--- a/solution.py
+++ b/solution.py
@@ -12,7 +12,8 @@
 LOOP = 5
 VMEM_BYTES = 64 * 1024 * 1024 - 256 * 1024
 
-Y0, Z0, Z1, MOB, LAB, INV = range(6)
+STEPS = 3
+MOB, LAB, INV = range(STEPS, STEPS + 3)
 
 
 def farthest_first(n):
@@ -34,14 +35,12 @@
     step_out,
     mob,
     x0,
-    y0,
-    z0,
-    z1,
-    p0,
-    p1,
-    p2,
+    field,
+    direction,
+    history,
     rhs,
     lab,
+    inv_in,
     inv,
     inv_far,
     fx,
@@ -66,6 +65,7 @@
     lzs,
     lzh,
     lzf,
+    yrim_x,
     yrim_y,
     yrim_z,
     prim_y,
@@ -97,19 +97,18 @@
         ("gy", gy > 0, gy - 1),
         ("gy", gy < ny - 1, gy + 1),
     )
-    fields = {Y0: y0, Z0: z0, Z1: z1, MOB: mob}
 
     loads = [
         pltpu.make_async_copy(rhs_hbm, rhs, in_sem.at[0]),
         pltpu.make_async_copy(lab_hbm, lab, in_sem.at[1]),
         pltpu.make_async_copy(mob_hbm, mob.at[pl.ds(1, cx)], in_sem.at[2]),
-        pltpu.make_async_copy(inv_hbm, inv, in_sem.at[3]),
+        pltpu.make_async_copy(inv_hbm, inv_in, in_sem.at[3]),
     ]
     for load in loads:
         load.start()
 
     def clear(ref, *index):
-        ref[index] = jnp.zeros(ref.shape[len(index) :], ref.dtype)
+        ref[index or Ellipsis] = jnp.zeros(ref.shape[len(index) :], ref.dtype)
 
     for low in range(2):
 
@@ -117,37 +116,36 @@
         def _():
             clear(mob, cx + 1 if low else 0)
             clear(lxh, low)
-            for e in (Y0, Z0, Z1):
+            for e in range(STEPS):
                 clear(xh, e, low)
 
         @pl.when(gz == (nz - 1 if low else 0))
         def _():
             clear(lyh, low)
-            for e in (Y0, Z0, Z1, MOB):
+            for e in range(STEPS + 1):
                 clear(yh, e, low)
 
         @pl.when(gy == (ny - 1 if low else 0))
         def _():
             clear(lzh, low)
-            for e in (Y0, Z0, Z1, MOB):
+            for e in range(STEPS + 1):
                 clear(zh, e, low)
 
     barrier = pltpu.get_barrier_semaphore()
     plane_peers = [
-        {"gy": lax.rem(gy + j, ny), "gz": lax.rem(gz + k, nz)}
+        {"gx": lax.rem(gx + k, nx), "gy": lax.rem(gy + j, ny)}
+        for k in farthest_first(nx)
         for j in farthest_first(ny)
-        for k in farthest_first(nz)
         if j or k
     ]
-    line_peers = [{"gx": lax.rem(gx + k, nx)} for k in farthest_first(nx) if k]
-    phases = ((gy * nz + gz, plane_peers), (gx, line_peers))
+    line_peers = [{"gz": lax.rem(gz + k, nz)} for k in farthest_first(nz) if k]
+    phases = ((gy * nx + gx, plane_peers), (gz, line_peers))
     partners = plane_peers + line_peers
     for partner in partners:
         pl.semaphore_signal(barrier, inc=1, device_id=partner, device_id_type=MESH)
 
-    for field in (y0, z0, z1):
-        clear(field, 0)
-        clear(field, cx + 1)
+    clear(field, 0)
+    clear(field, cx + 1)
 
     lane8 = lax.broadcasted_iota(jnp.int32, (8, 128), 1)
     row8 = lax.broadcasted_iota(jnp.int32, (8, 128), 0)
@@ -167,9 +165,10 @@
     def halo_copy(e, side):
         axis, _, index = sides[side]
         low, other = side & 1, 1 - (side & 1)
-        if e == INV:
+        kind = e if isinstance(e, int) else 0
+        if kind == INV:
             src, dst = inv, inv_far.at[side ^ 1]
-        elif e == LAB:
+        elif kind == LAB:
             if axis == "gx":
                 src, dst = lab.at[cx - 1 if low else 0], lxh.at[other]
             elif axis == "gz":
@@ -177,8 +176,8 @@
             else:
                 src, dst = lzs, lzh.at[other]
         elif axis == "gx":
-            src = fields[e].at[cx if low else 1]
-            dst = mob.at[0 if low else cx + 1] if e == MOB else xh.at[e, other]
+            src = (mob if kind == MOB else field).at[cx if low else 1]
+            dst = mob.at[0 if low else cx + 1] if kind == MOB else xh.at[e, other]
         elif axis == "gz":
             src, dst = ys.at[e, low], yh.at[e, other]
         else:
@@ -194,12 +193,13 @@
 
     def halo_landed(e, side):
         low = side & 1
-        if e == INV:
+        kind = e if isinstance(e, int) else 0
+        if kind == INV:
             ref = inv_far.at[side]
-        elif e == LAB:
+        elif kind == LAB:
             ref = (lxh, lyh, lzh)[side // 2].at[low]
         elif side < 2:
-            ref = mob.at[cx + 1 if low else 0] if e == MOB else xh.at[e, low]
+            ref = mob.at[cx + 1 if low else 0] if kind == MOB else xh.at[e, low]
         else:
             ref = (yh, zh)[side // 2 - 1].at[e, low]
         return pltpu.make_async_copy(ref, ref, hr_sem.at[e, side])
@@ -267,7 +267,7 @@
         tiles[7] = tiles[7] + jnp.where(row8 == 7, last, 0.0)
         return jnp.concatenate(tiles, axis=0)
 
-    def apply_all(field, body, init, outer, make=None):
+    def apply_all(values, body, init, outer, make=None):
         def step(x, carry, above_v):
             below, v, rest = carry
             above = fx[x + 1] * (above_v - v)
@@ -284,14 +284,14 @@
         if make is None:
 
             def make(x):
-                return field[x + 1]
+                return values[x + 1]
 
         v = make(0)
-        carry = (fx[0] * (v - field[0]), v, init)
+        carry = (fx[0] * (v - values[0]), v, init)
         carry = lax.fori_loop(
             0, cx - 1, lambda x, c: step(x, c, make(x + 1)), carry, unroll=LOOP
         )
-        return step(cx - 1, carry, field[cx + 1])[2]
+        return step(cx - 1, carry, values[cx + 1])[2]
 
     def subset_sums(values, bits):
         terms = [values]
@@ -342,25 +342,27 @@
             tiles = merged
         return tiles[0]
 
-    def placed(sums, block):
-        rows = jnp.concatenate([rows_of(list(sums[:8])), rows_of(list(sums[8:]))], axis=0)
-        column = jnp.sum(rows, axis=1, keepdims=True)
-        return fold(jnp.where(lane16 == 16 * block + row16, column, 0.0))
-
-    def make_tile(sums, parts, dots):
-        tiles = [placed(sums, gz) + placed(parts[2], gz - 1) + placed(parts[3], gz + 1)]
-        for side in (4, 5, 0, 1):
-            tiles.append(placed(parts[side], gz))
-        narrow = []
-        for dot in dots:
-            dot = dot + pltpu.roll(dot, 64, 1)
-            narrow.append(dot + pltpu.roll(dot, 32, 1))
-        joined = zero
-        for k, dot in enumerate(narrow):
-            joined = jnp.where(lane8 >> 5 == k, dot, joined)
-        return rows_of(tiles + [joined, zero, zero])[:6]
-
-    def neighbour_parts(e, field):
+    def message(groups, dots):
+        tiles = []
+        for sums in groups:
+            tiles += [rows_of(list(sums[:8])), rows_of(list(sums[8:]))]
+        if dots:
+            tiles.append(rows_of(list(dots) + [zero] * (8 - len(dots))))
+        line = zero
+        for k, tile in enumerate(tiles):
+            column = jnp.sum(tile, axis=1, keepdims=True)
+            line = line + jnp.where(lane8 == 8 * k + row8, column, 0.0)
+        return jnp.sum(line, axis=0, keepdims=True)
+
+    def transpose_groups(tile):
+        for s in (4, 2, 1):
+            group = (lane8 >> 4) & s
+            up = pltpu.roll(pltpu.roll(tile, 8 - s, 0), 16 * s, 1)
+            down = pltpu.roll(pltpu.roll(tile, s, 0), 128 - 16 * s, 1)
+            tile = jnp.where((row8 & s) == group, tile, jnp.where(group != 0, up, down))
+        return tile
+
+    def neighbour_parts(e):
         parts = [
             by_label(lxh[0], -(fx[0] * field[1])),
             by_label(lxh[1], -(fx[cx] * field[cx])),
@@ -375,22 +377,24 @@
             parts.append([a + b for a, b in zip(*halves)])
         return parts
 
-    def coarse_right_side(e, field):
+    def coarse_right_side(e):
         sums = apply_all(
             field, lambda x, v, out, s: restrict_plane(x, out, s), no_sums, lambda x, v: rim[x] * v
         )
-        return label_sums(sums), neighbour_parts(e, field)
+        return label_sums(sums), neighbour_parts(e)
 
     def slots_of(g, ph):
-        if g == 0:
-            return (G1_first, G2_first)[ph]
-        if g == 4:
-            return (G1_last, G2_last)[ph]
+        if isinstance(g, int):
+            return ((G1_first, G2_first), (G1_last, G2_last))[g != 0][ph]
         return (G1, G2)[ph].at[g - 1]
+
+    def phase_slots(g, ph, first, count):
+        slots = slots_of(g, ph)
+        return slots.at[pl.ds(first, count)]
 
     def phase_start(g, ph):
         me, peers = phases[ph]
-        slot = slots_of(g, ph).at[me]
+        slot = phase_slots(g, ph, me, 1)
         for peer in peers:
             pltpu.make_async_remote_copy(
                 src_ref=slot,
@@ -402,7 +406,7 @@
             ).start()
 
     def phase_wait(g, ph):
-        part = slots_of(g, ph).at[pl.ds(0, len(phases[ph][1]))]
+        part = phase_slots(g, ph, 0, len(phases[ph][1]))
         pltpu.make_async_copy(part, part, gr_sem.at[g, ph]).wait()
         pltpu.make_async_copy(part, part, gs_sem.at[g, ph]).wait()
 
@@ -412,23 +416,32 @@
     def shift_up(rows):
         return jnp.concatenate([rows[1:], jnp.zeros((1, 128), F32)], axis=0)
 
-    def line_sums(slots):
-        return [jnp.sum(slots[j * nz : (j + 1) * nz], axis=0) for j in range(ny)]
-
-    def gather(g, tile):
-        G1[g - 1, gy * nz + gz] = tile
+    def group_lines(slots):
+        tiles = [transpose_groups(slots[nx * j : nx * (j + 1)]) for j in range(ny)]
+
+        def pick(group):
+            return jnp.concatenate([tile[group : group + 1] for tile in tiles], axis=0)
+
+        return pick
+
+    lane4 = lax.broadcasted_iota(jnp.int32, (ny, 128), 1)
+
+    def gather(g, line, started, between):
+        G1[g - 1, pl.ds(gy * nx + gx, 1), :] = line
         phase_start(g, 0)
+        started()
         phase_wait(g, 0)
-        lines = line_sums(G1[g - 1])
-
-        def pick(row):
-            return jnp.concatenate([line[row : row + 1] for line in lines], axis=0)
-
-        G2[g - 1, gx, 0:ny] = pick(0) + shift_down(pick(2)) + shift_up(pick(1))
-        G2[g - 1, gx, ny : 2 * ny] = pick(3)
-        G2[g - 1, gx, 2 * ny : 3 * ny] = pick(4)
-        G2[g - 1, gx, 3 * ny : 3 * ny + 1] = sum(lines[1:], lines[0])[5:6]
+        pick = group_lines(G1.at[g - 1])
+        own = pick(0)
+        own = own + jnp.where(lane4 < 112, pltpu.roll(pick(1), 112, 1), 0.0)
+        own = own + jnp.where(lane4 >= 16, pltpu.roll(pick(2), 16, 1), 0.0)
+        own = own + shift_up(pick(3)) + shift_down(pick(4))
+        G2[g - 1, gz, 0:ny] = own
+        G2[g - 1, gz, ny : 2 * ny] = pick(5)
+        G2[g - 1, gz, 2 * ny : 3 * ny] = pick(6)
+        G2[g - 1, gz, 3 * ny : 3 * ny + 1] = jnp.sum(pick(7), axis=0, keepdims=True)
         phase_start(g, 1)
+        between()
         phase_wait(g, 1)
 
     def dots_of(g):
@@ -436,18 +449,18 @@
         lane = lax.broadcasted_iota(jnp.int32, (1, 128), 1)
         return [
             jnp.broadcast_to(
-                jnp.sum(jnp.where(lane >> 5 == k, row, 0.0), axis=1, keepdims=True), (1, 128)
+                jnp.sum(jnp.where(lane & 15 == k, row, 0.0), axis=1, keepdims=True), (1, 128)
             )
             for k in range(3)
         ]
 
     def right_side(g):
-        if g == 0:
-            return [G2_first[i] for i in range(nx)]
+        if isinstance(g, int):
+            return [G2_first[i] for i in range(nz)]
         blocks = []
-        for i in range(nx):
+        for i in range(nz):
             rows = G2[g - 1, i, 0:ny]
-            if i + 1 < nx:
+            if i + 1 < nz:
                 rows = rows + G2[g - 1, i + 1, ny : 2 * ny]
             if i > 0:
                 rows = rows + G2[g - 1, i - 1, 2 * ny : 3 * ny]
@@ -499,11 +512,25 @@
     loads[0].wait()
     loads[1].wait()
     sums = lax.fori_loop(0, cx, restrict_rhs, no_sums, unroll=4)
-    line = jnp.sum(placed(label_sums(sums), gz), axis=0, keepdims=True)
+    line = message([label_sums(sums)], ())
     pl.semaphore_wait(barrier, len(partners))
-    G1_first[gy * nz + gz] = line
+    G1_first[pl.ds(gy * nx + gx, 1), :] = line
     phase_start(0, 0)
     loads[2].wait()
+
+    def order_columns():
+        for top in (0, 8):
+            for j in range(ny):
+                tiles = [inv_in[top : top + 8, pl.ds((i * ny + j) * 128, 128)] for i in range(nx)]
+                for s in (4, 2, 1):
+                    clear_bit = (lane8 >> 4) & s == 0
+                    for i in range(nx):
+                        if not i & s:
+                            a, b = tiles[i], tiles[i | s]
+                            tiles[i] = jnp.where(clear_bit, a, pltpu.roll(b, 16 * s, 1))
+                            tiles[i | s] = jnp.where(clear_bit, pltpu.roll(a, 128 - 16 * s, 1), b)
+                for i in range(nz):
+                    inv[top : top + 8, pl.ds((i * ny + j) * 128, 128)] = tiles[i]
 
     def stage_static(x, carry):
         stage_plane(MOB, x, mob[x + 1])
@@ -519,9 +546,12 @@
     exchange_start(MOB)
     exchange_start(LAB)
     loads[3].wait()
+    order_columns()
     exchange_start(INV)
 
     def faces():
+        for ref in (direction, ws, yrim_x, yrim_y, yrim_z, prim_y, prim_z):
+            clear(ref)
         exchange_wait(MOB)
         exchange_wait(LAB)
         for half in range(2):
@@ -557,8 +587,7 @@
         lax.fori_loop(0, cx, step, fx[0], unroll=4)
 
     phase_wait(0, 0)
-    for j, row in enumerate(line_sums(G1_first)):
-        G2_first[gx, j : j + 1] = row
+    G2_first[gz] = group_lines(G1_first)(0)
     phase_start(0, 1)
     faces()
     phase_wait(0, 1)
@@ -580,38 +609,50 @@
         residual = rhs[x] - out
         precond = residual * dinv[x]
         rs[x] = residual
-        y0[x + 1] = precond
-        stage_plane(Y0, x, precond)
+        field[x + 1] = precond
+        stage_plane(0, x, precond)
         return dot + fold(residual * precond)
 
     ry_part = apply_all(x0, first_residual, zero, edge_part, first_iterate)
-    stage_end(Y0)
-    exchange_start(Y0)
-    sums, parts = coarse_right_side(Y0, y0)
-    gather(1, make_tile(sums, parts, (ry_part,)))
-    lines = coarse(1)
-    ry = dots_of(1)[0]
-
-    def first_direction(x):
-        plane = y0[x + 1] - take(line_here, lab[x])
-        p0[x + 1] = plane
-        return plane
-
-    line_here = lines[6]
-    direction = first_direction
-    exchange_wait(Y0)
-    x_far, y_own, y_far, z_own, z_far = rim_of(lines)
-    for low in range(2):
-        p0[cx + 1 if low else 0] = xh[Y0, low] - x_far[low]
-        yrim_y[low] = ys[Y0, low]
-        yrim_y[2 + low] = yh[Y0, low]
-        yrim_z[low] = zs[Y0, low]
-        yrim_z[2 + low] = far(zh.at[Y0], low)
-    for k, (y_part, z_part) in enumerate(zip(y_own + y_far, z_own + z_far)):
-        prim_y[k] = yrim_y[k] - y_part
-        prim_z[k] = yrim_z[k] - z_part
-
-    def prim_faces():
+    stage_end(0)
+
+    def tall(row):
+        return jnp.broadcast_to(row, (8, 128))
+
+    def one_step(k, carry):
+        ry, lines, dots, _, last_alpha = carry
+        ry, lines = ry[0:1], [line[0:1] for line in lines]
+        sums, parts = coarse_right_side(k)
+        gather(
+            k + 1,
+            message([sums] + [parts[side] for side in (0, 1, 4, 5, 2, 3)], dots),
+            lambda: exchange_start(k),
+            lambda: exchange_wait(k),
+        )
+        more = coarse(k + 1)
+        d0, d1, d2 = dots_of(k + 1)
+        first = lax.broadcasted_iota(jnp.int32, (1, 128), 0) + k == 0
+        alpha = jnp.where(first, 0.0, ry / d0)
+        ry_next = jnp.where(first, d0, ry + alpha * (alpha * d2 - 2.0 * d1))
+        beta = jnp.where(first, 0.0, ry_next / ry)
+        gain = jnp.where(first, 1.0, -alpha)
+        lines = [line + gain * extra for line, extra in zip(lines, more)]
+
+        x_far, y_own, y_far, z_own, z_far = rim_of(lines)
+        for low in range(2):
+            outer = cx + 1 if low else 0
+            layer = yrim_x[low] + gain * xh[k, low]
+            yrim_x[low] = layer
+            direction[outer] = (layer + beta * direction[outer]) - x_far[low]
+        rows = [ys[k, 0], ys[k, 1], yh[k, 0], yh[k, 1]]
+        packs = [zs[k, 0], zs[k, 1], far(zh.at[k], 0), far(zh.at[k], 1)]
+        for i, (y_part, z_part) in enumerate(zip(y_own + y_far, z_own + z_far)):
+            row = yrim_y[i] + gain * rows[i]
+            pack = yrim_z[i] + gain * packs[i]
+            yrim_y[i] = row
+            yrim_z[i] = pack
+            prim_y[i] = (row + beta * prim_y[i]) - y_part
+            prim_z[i] = (pack + beta * prim_z[i]) - z_part
         outer_faces(
             [prim_y[0], prim_y[1]],
             [prim_y[2], prim_y[3]],
@@ -619,92 +660,56 @@
             [prim_z[2], prim_z[3]],
         )
 
-    prim_faces()
-
-    alphas = []
-    for g, here, scaled, e, after in ((2, p0, z0, Z0, p1), (3, p1, z1, Z1, p2)):
+        def next_direction(x):
+            residual = rs[x] - alpha * ws[x]
+            rs[x] = residual
+            plane = (residual * dinv[x] + beta * direction[x + 1]) - take(lines[6], lab[x])
+            direction[x + 1] = plane
+            history[k, x] = plane
+            return plane
 
         def image(x, v, out, dots):
             z = out * dinv[x]
             ws[x] = out
-            scaled[x + 1] = z
-            stage_plane(e, x, z)
+            field[x + 1] = z
+            stage_plane(k + 1, x, z)
             return (
                 dots[0] + fold(v * out),
                 dots[1] + fold(rs[x] * z),
                 dots[2] + fold(out * z),
             )
 
-        dots = apply_all(here, image, (zero, zero, zero), edge_part, direction)
-        stage_end(e)
-        exchange_start(e)
-        sums, parts = coarse_right_side(e, scaled)
-        gather(g, make_tile(sums, parts, dots))
-        more = coarse(g)
-        pw, rz, wz = dots_of(g)
-        alpha = ry / pw
-        alphas.append(alpha)
-        ry_next = ry + alpha * (alpha * wz - 2.0 * rz)
-        beta = ry_next / ry
-        ry = ry_next
-        lines = [line - alpha * extra for line, extra in zip(lines, more)]
-
-        def next_direction(x, here=here, after=after, alpha=alpha, beta=beta, line=lines[6]):
-            p = here[x + 1]
-            residual = rs[x] - alpha * ws[x]
-            rs[x] = residual
-            plane = (residual * dinv[x] + beta * p) - take(line, lab[x])
-            after[x + 1] = plane
-            return plane
-
-        direction = next_direction
-        exchange_wait(e)
-        x_far, y_own, y_far, z_own, z_far = rim_of(lines)
-        for low in range(2):
-            outer = cx + 1 if low else 0
-            layer = xh[Y0, low] - alpha * xh[e, low]
-            xh[Y0, low] = layer
-            after[outer] = (layer + beta * here[outer]) - x_far[low]
-        z_rows = [ys[e, 0], ys[e, 1], yh[e, 0], yh[e, 1]]
-        z_packs = [zs[e, 0], zs[e, 1], far(zh.at[e], 0), far(zh.at[e], 1)]
-        for k, (y_part, z_part) in enumerate(zip(y_own + y_far, z_own + z_far)):
-            rows = yrim_y[k] - alpha * z_rows[k]
-            packs = yrim_z[k] - alpha * z_packs[k]
-            yrim_y[k] = rows
-            yrim_z[k] = packs
-            prim_y[k] = (rows + beta * prim_y[k]) - y_part
-            prim_z[k] = (packs + beta * prim_z[k]) - z_part
-        prim_faces()
+        dots = apply_all(direction, image, (zero, zero, zero), edge_part, next_direction)
+        stage_end(k + 1)
+        return tall(ry_next), [tall(line) for line in lines], dots, last_alpha, tall(alpha)
+
+    ry, _, dots, *alphas = lax.fori_loop(
+        0, STEPS, one_step, (zero + 1.0, [zero] * 7, (ry_part, zero, zero), zero, zero)
+    )
+    ry, alphas = ry[0:1], [alpha[0:1] for alpha in alphas]
 
     stores = [
         pltpu.make_async_copy(xs, x_hbm, out_sem.at[0]),
-        pltpu.make_async_copy(p2.at[pl.ds(1, cx)], p_hbm, out_sem.at[1]),
+        pltpu.make_async_copy(history.at[STEPS - 1], p_hbm, out_sem.at[1]),
         pltpu.make_async_copy(rs, r_hbm, out_sem.at[2]),
         pltpu.make_async_copy(ws, w_hbm, out_sem.at[3]),
     ]
-
-    def last_image(x, v, out, dot):
-        ws[x] = out
-        return dot + fold(v * out)
-
-    part = apply_all(p2, last_image, zero, edge_part, direction)
-    last_tile = jnp.sum(part, axis=0, keepdims=True)
-    G1_last[gy * nz + gz] = last_tile
-    phase_start(4, 0)
+    G1_last[pl.ds(gy * nx + gx, 1), :] = jnp.sum(dots[0], axis=0, keepdims=True)
+    phase_start(STEPS + 1, 0)
     for store in stores[1:]:
         store.start()
 
     def join_iterate(x, carry):
-        xs[x] = (x0[x + 1] + alphas[0] * p0[x + 1]) + alphas[1] * p1[x + 1]
+        xs[x] = (x0[x + 1] + alphas[0] * history[0, x]) + alphas[1] * history[1, x]
         return carry
 
     lax.fori_loop(0, cx, join_iterate, 0, unroll=4)
     stores[0].start()
-    phase_wait(4, 0)
-    G2_last[gx] = jnp.sum(G1_last[...], axis=0)
-    phase_start(4, 1)
-    phase_wait(4, 1)
-    total = jnp.sum(jnp.sum(G2_last[...], axis=0), axis=1, keepdims=True)
+    phase_wait(STEPS + 1, 0)
+    G2_last[pl.ds(gz, 1), :] = jnp.sum(G1_last[...], axis=0, keepdims=True)
+    phase_start(STEPS + 1, 1)
+    phase_wait(STEPS + 1, 1)
+    total = jnp.sum(jnp.sum(G2_last[...], axis=0, keepdims=True), axis=1, keepdims=True)
     step_out[...] = jnp.broadcast_to(ry / total, step_out.shape)
     for store in stores:
         store.wait()
@@ -728,9 +733,11 @@
             in_specs=[hbm] * 4,
             out_specs=[hbm] * 4 + [pl.BlockSpec(memory_space=pltpu.VMEM)],
             scratch_shapes=[
-                *[vmem(cx + 2, cy, cz) for _ in range(8)],
+                *[vmem(cx + 2, cy, cz) for _ in range(4)],
+                vmem(STEPS, cx, cy, cz),
                 vmem(cx, cy, cz),
                 vmem(cx, cy, cz, dtype=i32),
+                vmem(*coarse_inverse.shape),
                 vmem(*coarse_inverse.shape),
                 vmem(6, *coarse_inverse.shape),
                 vmem(cx + 1, cy, cz),
@@ -739,7 +746,7 @@
                 vmem(2, cx, cz),
                 vmem(2, 8, 128),
                 *[vmem(cx, cy, cz) for _ in range(3)],
-                vmem(3, 2, cy, cz),
+                vmem(STEPS, 2, cy, cz),
                 vmem(4, 2, cx, cz),
                 vmem(4, 2, cx, cz),
                 vmem(4, 2, 8, 128),
@@ -750,6 +757,7 @@
                 vmem(2, 8, 128, dtype=i32),
                 vmem(2, 2, 8, 128, dtype=i32),
                 vmem(2, 8, 128, dtype=i32),
+                vmem(2, cy, cz),
                 vmem(4, cx, cz),
                 vmem(4, 8, 128),
                 vmem(4, cx, cz),
@@ -758,12 +766,12 @@
                 vmem(cx, 8, 128, dtype=i32),
                 vmem(cx, 8, 128),
                 vmem(2, cx, cz),
-                vmem(ny * nz, 1, 128),
-                vmem(nx, ny, 128),
-                vmem(3, ny * nz, 6, 128),
-                vmem(3, nx, 3 * ny + 1, 128),
-                vmem(ny * nz, 1, 128),
-                vmem(nx, 1, 128),
+                vmem(ny * nx, 128),
+                vmem(nz, ny, 128),
+                vmem(STEPS, ny * nx, 128),
+                vmem(STEPS, nz, 3 * ny + 1, 128),
+                vmem(ny * nx, 128),
+                vmem(nz, 128),
                 pltpu.SemaphoreType.DMA((4,)),
                 pltpu.SemaphoreType.DMA((4,)),
                 pltpu.SemaphoreType.DMA((6, 6)),

time: 76.8 us -> 76.5 us (level)
  no operation moved by 1% of the time
where the time goes in v2:
time: 76.5 us; the launch traced here: 76.4 us
  Pallas kernels  73 us (95%)
  other arithmetic  2.72 us (4%)
    pallas_call x1, Pallas kernels, per_device(): pl.pallas_call(functools.partial(kernel, nx, ny, nz), out_shape=[jax.Shap...  73 us
    sub x1, other arithmetic, per_device(): return (xs + alpha * p, rs - alpha * w)  2.72 us

profile of v2, /device:TPU:1, one launch (start us, length us, event | category | flops | bytes accessed | tf_op | source)
XLA Modules:
  0.0 76.4 jit_solution(9488700227037034878)
XLA Ops:
  0.6 73.0 %deflated_cg.1 = (f32[16,64,128]{2,1,0:T(8,128)}, f32[16,64,128]{2,1,0:T(8,128)}, f32[16,64,128]{2,1,0:T(8,128)}, f32[16,64,128]{2,1,0:T(8,128)}, f32[64,128]{1,0:T(8,128)}) custom-call(f32[16,64,128]{2,1,0:T(8,128)} %rhs_hbm.1, f32[16,64,128]{2,1,0:T(8,128)} %mob_hbm.1, s32[16,64,128]{2,1,0:T(8,128)} %lab_hbm.1, f32[16,4096]{1,0:T(8,128)} %inv_hbm.1), custom_call_target="tpu_custom_call" | custom-call | tf_op jit(solution)/shard_map/deflated_cg/pallas_call | solution.py:729
  73.6 2.7 %multiply_subtract_fusion = (f32[16,64,128]{2,1,0:T(8,128)}, f32[16,64,128]{2,1,0:T(8,128)}) fusion(f32[16,64,128]{2,1,0:T(8,128)} %get-tuple-element.10, f32[16,64,128]{2,1,0:T(8,128)} %get-tuple-element.11, f32[64,128]{1,0:T(8,128)} %get-tuple-element.8, f32[16,64,128]{2,1,0:T(8,128)} %get-tuple-element.7, f32[16,64,128]{2,1,0:T(8,128)} %get-tuple-element.9), kind=kLoop, calls=%fused_computation | loop fusion | flops 524288 | bytes 3178496 | tf_op jit(solution)/shard_map/sub | solution.py:787

commit v3 on v2

--- a/solution.py
+++ b/solution.py
@@ -7,7 +7,7 @@
 from jax.experimental.pallas import tpu as pltpu
 from jax.sharding import PartitionSpec as P
 
-MESH = pl.DeviceIdType.MESH
+LOGICAL = pl.DeviceIdType.LOGICAL
 F32 = jnp.float32
 LOOP = 5
 VMEM_BYTES = 64 * 1024 * 1024 - 256 * 1024
@@ -89,13 +89,16 @@
 ):
     cx = rhs.shape[0]
     gx, gy, gz = lax.axis_index("gx"), lax.axis_index("gy"), lax.axis_index("gz")
+    def logical(x, y, z):
+        return (lax.rem(x, nx) * ny + lax.rem(y, ny)) * nz + lax.rem(z, nz)
+
     sides = (
-        ("gx", gx > 0, gx - 1),
-        ("gx", gx < nx - 1, gx + 1),
-        ("gz", gz > 0, gz - 1),
-        ("gz", gz < nz - 1, gz + 1),
-        ("gy", gy > 0, gy - 1),
-        ("gy", gy < ny - 1, gy + 1),
+        ("gx", gx > 0, logical(gx + nx - 1, gy, gz)),
+        ("gx", gx < nx - 1, logical(gx + 1, gy, gz)),
+        ("gz", gz > 0, logical(gx, gy, gz + nz - 1)),
+        ("gz", gz < nz - 1, logical(gx, gy, gz + 1)),
+        ("gy", gy > 0, logical(gx, gy + ny - 1, gz)),
+        ("gy", gy < ny - 1, logical(gx, gy + 1, gz)),
     )
 
     loads = [
@@ -132,17 +135,24 @@
                 clear(zh, e, low)
 
     barrier = pltpu.get_barrier_semaphore()
+    chips = nz // 2
+    chip, core = lax.div(gz, 2), lax.rem(gz, 2)
+    line_peers = [
+        logical(gx + k, gy, 2 * chip + lax.rem(core + c, 2))
+        for k in farthest_first(nx)
+        for c in (1, 0)
+        if k or c
+    ]
     plane_peers = [
-        {"gx": lax.rem(gx + k, nx), "gy": lax.rem(gy + j, ny)}
-        for k in farthest_first(nx)
+        logical(gx, gy + j, gz + 2 * k)
         for j in farthest_first(ny)
+        for k in farthest_first(chips)
         if j or k
     ]
-    line_peers = [{"gz": lax.rem(gz + k, nz)} for k in farthest_first(nz) if k]
-    phases = ((gy * nx + gx, plane_peers), (gz, line_peers))
-    partners = plane_peers + line_peers
+    phases = ((core * nx + gx, line_peers), (gy * chips + chip, plane_peers))
+    partners = line_peers + plane_peers + [logical(gx, gy, gz + nz - 1 + 2 * core)]
     for partner in partners:
-        pl.semaphore_signal(barrier, inc=1, device_id=partner, device_id_type=MESH)
+        pl.semaphore_signal(barrier, inc=1, device_id=partner, device_id_type=LOGICAL)
 
     clear(field, 0)
     clear(field, cx + 1)
@@ -187,8 +197,8 @@
             dst_ref=dst,
             send_sem=hs_sem.at[e, side],
             recv_sem=hr_sem.at[e, side ^ 1],
-            device_id={axis: index},
-            device_id_type=MESH,
+            device_id=index,
+            device_id_type=LOGICAL,
         )
 
     def halo_landed(e, side):
@@ -402,7 +412,7 @@
                 send_sem=gs_sem.at[g, ph],
                 recv_sem=gr_sem.at[g, ph],
                 device_id=peer,
-                device_id_type=MESH,
+                device_id_type=LOGICAL,
             ).start()
 
     def phase_wait(g, ph):
@@ -410,42 +420,37 @@
         pltpu.make_async_copy(part, part, gr_sem.at[g, ph]).wait()
         pltpu.make_async_copy(part, part, gs_sem.at[g, ph]).wait()
 
-    def shift_down(rows):
-        return jnp.concatenate([jnp.zeros((1, 128), F32), rows[: ny - 1]], axis=0)
-
-    def shift_up(rows):
-        return jnp.concatenate([rows[1:], jnp.zeros((1, 128), F32)], axis=0)
-
     def group_lines(slots):
-        tiles = [transpose_groups(slots[nx * j : nx * (j + 1)]) for j in range(ny)]
-
-        def pick(group):
-            return jnp.concatenate([tile[group : group + 1] for tile in tiles], axis=0)
-
-        return pick
-
-    lane4 = lax.broadcasted_iota(jnp.int32, (ny, 128), 1)
+        return [transpose_groups(slots[nx * c : nx * (c + 1)]) for c in range(2)]
 
     def gather(g, line, started, between):
-        G1[g - 1, pl.ds(gy * nx + gx, 1), :] = line
+        G1[g - 1, pl.ds(phases[0][0], 1), :] = line
         phase_start(g, 0)
         started()
         phase_wait(g, 0)
-        pick = group_lines(G1.at[g - 1])
+        tiles = group_lines(G1.at[g - 1])
+
+        def pick(group):
+            return jnp.concatenate([tile[group : group + 1] for tile in tiles], axis=0)
+
+        lane2 = lax.broadcasted_iota(jnp.int32, (2, 128), 1)
         own = pick(0)
-        own = own + jnp.where(lane4 < 112, pltpu.roll(pick(1), 112, 1), 0.0)
-        own = own + jnp.where(lane4 >= 16, pltpu.roll(pick(2), 16, 1), 0.0)
-        own = own + shift_up(pick(3)) + shift_down(pick(4))
-        G2[g - 1, gz, 0:ny] = own
-        G2[g - 1, gz, ny : 2 * ny] = pick(5)
-        G2[g - 1, gz, 2 * ny : 3 * ny] = pick(6)
-        G2[g - 1, gz, 3 * ny : 3 * ny + 1] = jnp.sum(pick(7), axis=0, keepdims=True)
+        own = own + jnp.where(lane2 < 112, pltpu.roll(pick(1), 112, 1), 0.0)
+        own = own + jnp.where(lane2 >= 16, pltpu.roll(pick(2), 16, 1), 0.0)
+        own = own + jnp.concatenate([tiles[1][5:6], tiles[0][6:7]], axis=0)
+        slot = phases[1][0]
+        G2[g - 1, slot, 0:2] = own
+        G2[g - 1, slot, 2:4] = pick(3)
+        G2[g - 1, slot, 4:6] = pick(4)
+        G2[g - 1, slot, 6:7] = tiles[0][5:6]
+        G2[g - 1, slot, 7:8] = tiles[1][6:7]
+        G2[g - 1, slot, 8:9] = tiles[0][7:8] + tiles[1][7:8]
         phase_start(g, 1)
         between()
         phase_wait(g, 1)
 
     def dots_of(g):
-        row = jnp.sum(G2[g - 1, :, 3 * ny : 3 * ny + 1], axis=0)
+        row = jnp.sum(G2[g - 1, :, 8:9], axis=0)
         lane = lax.broadcasted_iota(jnp.int32, (1, 128), 1)
         return [
             jnp.broadcast_to(
@@ -455,24 +460,33 @@
         ]
 
     def right_side(g):
-        if isinstance(g, int):
-            return [G2_first[i] for i in range(nz)]
-        blocks = []
-        for i in range(nz):
-            rows = G2[g - 1, i, 0:ny]
-            if i + 1 < nz:
-                rows = rows + G2[g - 1, i + 1, ny : 2 * ny]
-            if i > 0:
-                rows = rows + G2[g - 1, i - 1, 2 * ny : 3 * ny]
-            blocks.append(rows)
-        return blocks
+        rows = [[None] * ny for _ in range(nz)]
+        for j in range(ny):
+            for k in range(chips):
+                slot = j * chips + k
+                if isinstance(g, int):
+                    pairs = G2_first[slot]
+                    low, high = pairs[0:1], pairs[1:2]
+                else:
+                    pairs = G2[g - 1, slot, 0:2]
+                    if j + 1 < ny:
+                        pairs = pairs + G2[g - 1, slot + chips, 2:4]
+                    if j > 0:
+                        pairs = pairs + G2[g - 1, slot - chips, 4:6]
+                    low, high = pairs[0:1], pairs[1:2]
+                    if k > 0:
+                        low = low + G2[g - 1, slot - 1, 7:8]
+                    if k + 1 < chips:
+                        high = high + G2[g - 1, slot + 1, 6:7]
+                rows[2 * k][j], rows[2 * k + 1][j] = low, high
+        return rows
 
     def coarse(g):
         accs = [jnp.zeros((16, 128), F32) for _ in range(7)]
         for i, rows in enumerate(right_side(g)):
             for j in range(ny):
                 columns = slice((i * ny + j) * 128, (i * ny + j + 1) * 128)
-                row = rows[j : j + 1]
+                row = rows[j]
                 accs[6] = accs[6] + inv[:, columns] * row
                 for side in range(6):
                     accs[side] = accs[side] + inv_far[side, :, columns] * row
@@ -514,7 +528,7 @@
     sums = lax.fori_loop(0, cx, restrict_rhs, no_sums, unroll=4)
     line = message([label_sums(sums)], ())
     pl.semaphore_wait(barrier, len(partners))
-    G1_first[pl.ds(gy * nx + gx, 1), :] = line
+    G1_first[pl.ds(phases[0][0], 1), :] = line
     phase_start(0, 0)
     loads[2].wait()
 
@@ -587,7 +601,9 @@
         lax.fori_loop(0, cx, step, fx[0], unroll=4)
 
     phase_wait(0, 0)
-    G2_first[gz] = group_lines(G1_first)(0)
+    G2_first[phases[1][0]] = jnp.concatenate(
+        [tile[0:1] for tile in group_lines(G1_first)], axis=0
+    )
     phase_start(0, 1)
     faces()
     phase_wait(0, 1)
@@ -694,7 +710,7 @@
         pltpu.make_async_copy(rs, r_hbm, out_sem.at[2]),
         pltpu.make_async_copy(ws, w_hbm, out_sem.at[3]),
     ]
-    G1_last[pl.ds(gy * nx + gx, 1), :] = jnp.sum(dots[0], axis=0, keepdims=True)
+    G1_last[pl.ds(phases[0][0], 1), :] = jnp.sum(dots[0], axis=0, keepdims=True)
     phase_start(STEPS + 1, 0)
     for store in stores[1:]:
         store.start()
@@ -706,7 +722,7 @@
     lax.fori_loop(0, cx, join_iterate, 0, unroll=4)
     stores[0].start()
     phase_wait(STEPS + 1, 0)
-    G2_last[pl.ds(gz, 1), :] = jnp.sum(G1_last[...], axis=0, keepdims=True)
+    G2_last[pl.ds(phases[1][0], 1), :] = jnp.sum(G1_last[...], axis=0, keepdims=True)
     phase_start(STEPS + 1, 1)
     phase_wait(STEPS + 1, 1)
     total = jnp.sum(jnp.sum(G2_last[...], axis=0, keepdims=True), axis=1, keepdims=True)
@@ -766,12 +782,12 @@
                 vmem(cx, 8, 128, dtype=i32),
                 vmem(cx, 8, 128),
                 vmem(2, cx, cz),
-                vmem(ny * nx, 128),
-                vmem(nz, ny, 128),
-                vmem(STEPS, ny * nx, 128),
-                vmem(STEPS, nz, 3 * ny + 1, 128),
-                vmem(ny * nx, 128),
-                vmem(nz, 128),
+                vmem(2 * nx, 128),
+                vmem(ny * nz // 2, 2, 128),
+                vmem(STEPS, 2 * nx, 128),
+                vmem(STEPS, ny * nz // 2, 9, 128),
+                vmem(2 * nx, 128),
+                vmem(ny * nz // 2, 128),
                 pltpu.SemaphoreType.DMA((4,)),
                 pltpu.SemaphoreType.DMA((4,)),
                 pltpu.SemaphoreType.DMA((6, 6)),

time: 76.5 us -> 76.3 us (level)
  no operation moved by 1% of the time
where the time goes in v3:
time: 76.3 us; the launch traced here: 76.2 us
  Pallas kernels  72.8 us (95%)
  other arithmetic  2.72 us (4%)
    pallas_call x1, Pallas kernels, per_device(): pl.pallas_call(functools.partial(kernel, nx, ny, nz), out_shape=[jax.Shap...  72.8 us
    sub x1, other arithmetic, per_device(): return (xs + alpha * p, rs - alpha * w)  2.72 us

profile of v3, /device:TPU:1, one launch (start us, length us, event | category | flops | bytes accessed | tf_op | source)
XLA Modules:
  0.0 76.2 jit_solution(5976785112185877368)
XLA Ops:
  0.6 72.8 %deflated_cg.1 = (f32[16,64,128]{2,1,0:T(8,128)}, f32[16,64,128]{2,1,0:T(8,128)}, f32[16,64,128]{2,1,0:T(8,128)}, f32[16,64,128]{2,1,0:T(8,128)}, f32[64,128]{1,0:T(8,128)}) custom-call(f32[16,64,128]{2,1,0:T(8,128)} %rhs_hbm.1, f32[16,64,128]{2,1,0:T(8,128)} %mob_hbm.1, s32[16,64,128]{2,1,0:T(8,128)} %lab_hbm.1, f32[16,4096]{1,0:T(8,128)} %inv_hbm.1), custom_call_target="tpu_custom_call" | custom-call | tf_op jit(solution)/shard_map/deflated_cg/pallas_call | solution.py:745
  73.5 2.7 %multiply_subtract_fusion = (f32[16,64,128]{2,1,0:T(8,128)}, f32[16,64,128]{2,1,0:T(8,128)}) fusion(f32[16,64,128]{2,1,0:T(8,128)} %get-tuple-element.10, f32[16,64,128]{2,1,0:T(8,128)} %get-tuple-element.11, f32[64,128]{1,0:T(8,128)} %get-tuple-element.8, f32[16,64,128]{2,1,0:T(8,128)} %get-tuple-element.7, f32[16,64,128]{2,1,0:T(8,128)} %get-tuple-element.9), kind=kLoop, calls=%fused_computation | loop fusion | flops 524288 | bytes 3178496 | tf_op jit(solution)/shard_map/sub | solution.py:803

commit v4 on v3

--- a/solution.py
+++ b/solution.py
@@ -38,6 +38,9 @@
     field,
     direction,
     history,
+    rhs_in,
+    lab_in,
+    mob_in,
     rhs,
     lab,
     inv_in,
@@ -51,7 +54,7 @@
     bits,
     fyb,
     fzp,
-    xs,
+    ordered,
     rs,
     ws,
     xh,
@@ -102,9 +105,9 @@
     )
 
     loads = [
-        pltpu.make_async_copy(rhs_hbm, rhs, in_sem.at[0]),
-        pltpu.make_async_copy(lab_hbm, lab, in_sem.at[1]),
-        pltpu.make_async_copy(mob_hbm, mob.at[pl.ds(1, cx)], in_sem.at[2]),
+        pltpu.make_async_copy(rhs_hbm, rhs_in, in_sem.at[0]),
+        pltpu.make_async_copy(lab_hbm, lab_in, in_sem.at[1]),
+        pltpu.make_async_copy(mob_hbm, mob_in, in_sem.at[2]),
         pltpu.make_async_copy(inv_hbm, inv_in, in_sem.at[3]),
     ]
     for load in loads:
@@ -165,6 +168,19 @@
     ends = (lane8 == 0) | (lane8 == 127)
     even = (lane8 & 1) == 0
     zero = jnp.zeros((8, 128), F32)
+
+    def interleaved(ref, x):
+        return jnp.concatenate([ref[x, pl.ds(k, 8, stride=8), :] for k in range(8)], axis=0)
+
+    def store_in_order(ref, x, plane):
+        for k in range(8):
+            ref[x, pl.ds(k, 8, stride=8), :] = plane[8 * k : 8 * k + 8]
+
+    def next_row(plane):
+        return jnp.concatenate([plane[8:], pltpu.roll(plane[:8], 7, 0)], axis=0)
+
+    def last_row(plane):
+        return jnp.concatenate([pltpu.roll(plane[56:], 1, 0), plane[:56]], axis=0)
 
     def fold(plane):
         tiles = [plane[k : k + 8] for k in range(0, plane.shape[0], 8)]
@@ -281,11 +297,11 @@
         def step(x, carry, above_v):
             below, v, rest = carry
             above = fx[x + 1] * (above_v - v)
-            flux_y = fy[x] * (pltpu.roll(v, 63, 0) - v)
+            flux_y = fy[x] * (next_row(v) - v)
             flux_z = fz[x] * (pltpu.roll(v, 127, 1) - v)
             out = (
                 (below - above)
-                + (pltpu.roll(flux_y, 1, 0) - flux_y)
+                + (last_row(flux_y) - flux_y)
                 + (pltpu.roll(flux_z, 1, 1) - flux_z)
                 + outer(x, v)
             )
@@ -328,10 +344,14 @@
         return tuple(total + extra for total, extra in zip(sums, more))
 
     def restrict_rhs(x, sums):
-        planes = bits_of(lab[x])
+        labels = interleaved(lab_in, x)
+        values = interleaved(rhs_in, x)
+        lab[x] = labels
+        rhs[x] = values
+        planes = bits_of(labels)
         for i in range(4):
             bits[i, x] = planes[i]
-        return tuple(total + extra for total, extra in zip(sums, subset_sums(rhs[x], planes)))
+        return tuple(total + extra for total, extra in zip(sums, subset_sums(values, planes)))
 
     no_sums = (zero,) * 16
 
@@ -547,7 +567,9 @@
                     inv[top : top + 8, pl.ds((i * ny + j) * 128, 128)] = tiles[i]
 
     def stage_static(x, carry):
-        stage_plane(MOB, x, mob[x + 1])
+        mobility = interleaved(mob_in, x)
+        mob[x + 1] = mobility
+        stage_plane(MOB, x, mobility)
         labels = lab[x]
         stage_rows(lys, x, labels)
         lt[x] = pack_plane(labels)
@@ -582,12 +604,12 @@
         def step(x, below):
             m = mob[x + 1]
             above = 0.5 * (mob[x + 2] + m)
-            face_y = jnp.where(row == 63, 0.0, 0.5 * (pltpu.roll(m, 63, 0) + m))
+            face_y = jnp.where(row == 63, 0.0, 0.5 * (next_row(m) + m))
             face_z = jnp.where(lane == 127, 0.0, 0.5 * (pltpu.roll(m, 127, 1) + m))
             edges = edge_tiles(x)
             diag = (
                 (below + above)
-                + (pltpu.roll(face_y, 1, 0) + face_y)
+                + (last_row(face_y) + face_y)
                 + (pltpu.roll(face_z, 1, 1) + face_z)
                 + edges
             )
@@ -705,22 +727,21 @@
     ry, alphas = ry[0:1], [alpha[0:1] for alpha in alphas]
 
     stores = [
-        pltpu.make_async_copy(xs, x_hbm, out_sem.at[0]),
-        pltpu.make_async_copy(history.at[STEPS - 1], p_hbm, out_sem.at[1]),
-        pltpu.make_async_copy(rs, r_hbm, out_sem.at[2]),
-        pltpu.make_async_copy(ws, w_hbm, out_sem.at[3]),
+        pltpu.make_async_copy(ordered.at[i], out, out_sem.at[i])
+        for i, out in enumerate((x_hbm, p_hbm, r_hbm, w_hbm))
     ]
     G1_last[pl.ds(phases[0][0], 1), :] = jnp.sum(dots[0], axis=0, keepdims=True)
     phase_start(STEPS + 1, 0)
-    for store in stores[1:]:
+
+    def join_iterate(x, carry):
+        joined = (x0[x + 1] + alphas[0] * history[0, x]) + alphas[1] * history[1, x]
+        for i, plane in enumerate((joined, history[STEPS - 1, x], rs[x], ws[x])):
+            store_in_order(ordered.at[i], x, plane)
+        return carry
+
+    lax.fori_loop(0, cx, join_iterate, 0, unroll=4)
+    for store in stores:
         store.start()
-
-    def join_iterate(x, carry):
-        xs[x] = (x0[x + 1] + alphas[0] * history[0, x]) + alphas[1] * history[1, x]
-        return carry
-
-    lax.fori_loop(0, cx, join_iterate, 0, unroll=4)
-    stores[0].start()
     phase_wait(STEPS + 1, 0)
     G2_last[pl.ds(phases[1][0], 1), :] = jnp.sum(G1_last[...], axis=0, keepdims=True)
     phase_start(STEPS + 1, 1)
@@ -753,6 +774,9 @@
                 vmem(STEPS, cx, cy, cz),
                 vmem(cx, cy, cz),
                 vmem(cx, cy, cz, dtype=i32),
+                vmem(cx, cy, cz),
+                vmem(cx, cy, cz),
+                vmem(cx, cy, cz, dtype=i32),
                 vmem(*coarse_inverse.shape),
                 vmem(*coarse_inverse.shape),
                 vmem(6, *coarse_inverse.shape),
@@ -761,7 +785,8 @@
                 vmem(4, cx, cy, cz),
                 vmem(2, cx, cz),
                 vmem(2, 8, 128),
-                *[vmem(cx, cy, cz) for _ in range(3)],
+                vmem(4, cx, cy, cz),
+                *[vmem(cx, cy, cz) for _ in range(2)],
                 vmem(STEPS, 2, cy, cz),
                 vmem(4, 2, cx, cz),
                 vmem(4, 2, cx, cz),

time: 76.3 us -> 76.1 us (level)
  no operation moved by 1% of the time
where the time goes in v4:
time: 76.1 us; the launch traced here: 76 us
  Pallas kernels  72.6 us (95%)
  other arithmetic  2.72 us (4%)
    pallas_call x1, Pallas kernels, per_device(): pl.pallas_call(functools.partial(kernel, nx, ny, nz), out_shape=[jax.Shap...  72.6 us
    sub x1, other arithmetic, per_device(): return (xs + alpha * p, rs - alpha * w)  2.72 us

profile of v4, /device:TPU:1, one launch (start us, length us, event | category | flops | bytes accessed | tf_op | source)
XLA Modules:
  0.0 76.0 jit_solution(2475260463074032510)
XLA Ops:
  0.6 72.6 %deflated_cg.1 = (f32[16,64,128]{2,1,0:T(8,128)}, f32[16,64,128]{2,1,0:T(8,128)}, f32[16,64,128]{2,1,0:T(8,128)}, f32[16,64,128]{2,1,0:T(8,128)}, f32[64,128]{1,0:T(8,128)}) custom-call(f32[16,64,128]{2,1,0:T(8,128)} %rhs_hbm.1, f32[16,64,128]{2,1,0:T(8,128)} %mob_hbm.1, s32[16,64,128]{2,1,0:T(8,128)} %lab_hbm.1, f32[16,4096]{1,0:T(8,128)} %inv_hbm.1), custom_call_target="tpu_custom_call" | custom-call | tf_op jit(solution)/shard_map/deflated_cg/pallas_call | solution.py:766
  73.3 2.7 %multiply_subtract_fusion = (f32[16,64,128]{2,1,0:T(8,128)}, f32[16,64,128]{2,1,0:T(8,128)}) fusion(f32[16,64,128]{2,1,0:T(8,128)} %get-tuple-element.10, f32[16,64,128]{2,1,0:T(8,128)} %get-tuple-element.11, f32[64,128]{1,0:T(8,128)} %get-tuple-element.8, f32[16,64,128]{2,1,0:T(8,128)} %get-tuple-element.7, f32[16,64,128]{2,1,0:T(8,128)} %get-tuple-element.9), kind=kLoop, calls=%fused_computation | loop fusion | flops 524288 | bytes 3178496 | tf_op jit(solution)/shard_map/sub | solution.py:828

commit v5 on v4

--- a/solution.py
+++ b/solution.py
@@ -510,31 +510,37 @@
                 accs[6] = accs[6] + inv[:, columns] * row
                 for side in range(6):
                     accs[side] = accs[side] + inv_far[side, :, columns] * row
-        lines = []
+        values = []
         for side in range(7):
-            total = jnp.sum(accs[side], axis=1, keepdims=True)
-            line = jnp.sum(jnp.where(lane16 == row16, total, 0.0), axis=0, keepdims=True)
+            total = jnp.broadcast_to(jnp.sum(accs[side], axis=1, keepdims=True), (16, 128))
             if side < 6:
-                index = lax.broadcasted_iota(jnp.int32, (1, 128), 1) * 0 + (gx, gz, gy)[side // 2]
+                index = row16 * 0 + (gx, gz, gy)[side // 2]
                 edge = (0, (nx, nz, ny)[side // 2] - 1)[side & 1]
-                line = jnp.where(index == edge, 0.0, line)
-            lines.append(line)
-        return lines
-
-    def take(line, labels):
-        return jnp.take_along_axis(
-            jnp.broadcast_to(line, labels.shape), labels, axis=1, mode="promise_in_bounds"
-        )
-
-    def rim_of(lines):
-        x_far = [take(lines[low], lxh[low]) for low in range(2)]
-        y_own = [take(lines[6], lys[low]) for low in range(2)]
-        y_far = [take(lines[2 + low], lyh[low]) for low in range(2)]
-        z_own = [take(lines[6], lzs[half]) for half in range(2)]
-        z_far = [
-            jnp.where(even, take(lines[4], lzf[half]), take(lines[5], lzf[half]))
-            for half in range(2)
-        ]
+                total = jnp.where(index == edge, 0.0, total)
+            values.append(total)
+        return values
+
+    def take(values, masks):
+        picked = [jnp.broadcast_to(values[m : m + 1], masks[0].shape) for m in range(16)]
+        for mask in masks:
+            picked = [jnp.where(mask, b, a) for a, b in zip(picked[::2], picked[1::2])]
+        return picked[0]
+
+    def masks_of(labels):
+        return [labels & (1 << i) != 0 for i in range(4)]
+
+    def take_plane(values, x):
+        return take(values, [bits[i, x] > 0.5 for i in range(4)])
+
+    def rim_of(values):
+        x_far = [take(values[low], masks_of(lxh[low])) for low in range(2)]
+        y_own = [take(values[6], masks_of(lys[low])) for low in range(2)]
+        y_far = [take(values[2 + low], masks_of(lyh[low])) for low in range(2)]
+        z_own = [take(values[6], masks_of(lzs[half])) for half in range(2)]
+        z_far = []
+        for half in range(2):
+            masks = masks_of(lzf[half])
+            z_far.append(jnp.where(even, take(values[4], masks), take(values[5], masks)))
         return x_far, y_own, y_far, z_own, z_far
 
     def outer_faces(y_own, y_far, z_own, z_far):
@@ -634,7 +640,7 @@
     lines = coarse(0)
 
     def first_iterate(x):
-        plane = take(lines[6], lab[x])
+        plane = take_plane(lines[6], x)
         x0[x + 1] = plane
         return plane
 
@@ -659,7 +665,7 @@
 
     def one_step(k, carry):
         ry, lines, dots, _, last_alpha = carry
-        ry, lines = ry[0:1], [line[0:1] for line in lines]
+        ry = ry[0:1]
         sums, parts = coarse_right_side(k)
         gather(
             k + 1,
@@ -701,7 +707,7 @@
         def next_direction(x):
             residual = rs[x] - alpha * ws[x]
             rs[x] = residual
-            plane = (residual * dinv[x] + beta * direction[x + 1]) - take(lines[6], lab[x])
+            plane = (residual * dinv[x] + beta * direction[x + 1]) - take_plane(lines[6], x)
             direction[x + 1] = plane
             history[k, x] = plane
             return plane
@@ -719,10 +725,10 @@
 
         dots = apply_all(direction, image, (zero, zero, zero), edge_part, next_direction)
         stage_end(k + 1)
-        return tall(ry_next), [tall(line) for line in lines], dots, last_alpha, tall(alpha)
+        return tall(ry_next), lines, dots, last_alpha, tall(alpha)
 
     ry, _, dots, *alphas = lax.fori_loop(
-        0, STEPS, one_step, (zero + 1.0, [zero] * 7, (ry_part, zero, zero), zero, zero)
+        0, STEPS, one_step, (zero + 1.0, [jnp.zeros((16, 128), F32)] * 7, (ry_part, zero, zero), zero, zero)
     )
     ry, alphas = ry[0:1], [alpha[0:1] for alpha in alphas]
 

time: 76.1 us -> 74.2 us (0.975)
  Pallas kernels: 72.6 us -> 70.7 us
    pallas_call x1, Pallas kernels: 72.6 us -> 70.7 us  [per_device(): pl.pallas_call(functools.partial(kernel, nx, ny, nz), out_shape=[jax.Shap...]
where the time goes in v5:
time: 74.2 us; the launch traced here: 74.1 us
  Pallas kernels  70.7 us (95%)
  other arithmetic  2.72 us (4%)
    pallas_call x1, Pallas kernels, per_device(): pl.pallas_call(functools.partial(kernel, nx, ny, nz), out_shape=[jax.Shap...  70.7 us
    sub x1, other arithmetic, per_device(): return (xs + alpha * p, rs - alpha * w)  2.72 us

profile of v5, /device:TPU:1, one launch (start us, length us, event | category | flops | bytes accessed | tf_op | source)
XLA Modules:
  0.0 74.1 jit_solution(5126560576653134380)
XLA Ops:
  0.6 70.7 %deflated_cg.1 = (f32[16,64,128]{2,1,0:T(8,128)}, f32[16,64,128]{2,1,0:T(8,128)}, f32[16,64,128]{2,1,0:T(8,128)}, f32[16,64,128]{2,1,0:T(8,128)}, f32[64,128]{1,0:T(8,128)}) custom-call(f32[16,64,128]{2,1,0:T(8,128)} %rhs_hbm.1, f32[16,64,128]{2,1,0:T(8,128)} %mob_hbm.1, s32[16,64,128]{2,1,0:T(8,128)} %lab_hbm.1, f32[16,4096]{1,0:T(8,128)} %inv_hbm.1), custom_call_target="tpu_custom_call" | custom-call | tf_op jit(solution)/shard_map/deflated_cg/pallas_call | solution.py:772
  71.4 2.7 %multiply_subtract_fusion = (f32[16,64,128]{2,1,0:T(8,128)}, f32[16,64,128]{2,1,0:T(8,128)}) fusion(f32[16,64,128]{2,1,0:T(8,128)} %get-tuple-element.10, f32[16,64,128]{2,1,0:T(8,128)} %get-tuple-element.11, f32[64,128]{1,0:T(8,128)} %get-tuple-element.8, f32[16,64,128]{2,1,0:T(8,128)} %get-tuple-element.7, f32[16,64,128]{2,1,0:T(8,128)} %get-tuple-element.9), kind=kLoop, calls=%fused_computation | loop fusion | flops 524288 | bytes 3178496 | tf_op jit(solution)/shard_map/sub | solution.py:834

commit v6 on v5

--- a/solution.py
+++ b/solution.py
@@ -372,25 +372,20 @@
             tiles = merged
         return tiles[0]
 
-    def message(groups, dots):
-        tiles = []
-        for sums in groups:
-            tiles += [rows_of(list(sums[:8])), rows_of(list(sums[8:]))]
-        if dots:
-            tiles.append(rows_of(list(dots) + [zero] * (8 - len(dots))))
-        line = zero
-        for k, tile in enumerate(tiles):
-            column = jnp.sum(tile, axis=1, keepdims=True)
-            line = line + jnp.where(lane8 == 8 * k + row8, column, 0.0)
-        return jnp.sum(line, axis=0, keepdims=True)
-
-    def transpose_groups(tile):
-        for s in (4, 2, 1):
-            group = (lane8 >> 4) & s
-            up = pltpu.roll(pltpu.roll(tile, 8 - s, 0), 16 * s, 1)
-            down = pltpu.roll(pltpu.roll(tile, s, 0), 128 - 16 * s, 1)
-            tile = jnp.where((row8 & s) == group, tile, jnp.where(group != 0, up, down))
-        return tile
+    def placed(sums, block):
+        rows = jnp.concatenate([rows_of(list(sums[:8])), rows_of(list(sums[8:]))], axis=0)
+        column = jnp.sum(rows, axis=1, keepdims=True)
+        return fold(jnp.where(lane16 == 16 * block + row16, column, 0.0))
+
+    def message(sums, parts, dots):
+        tiles = [placed(sums, gx) + placed(parts[0], gx - 1) + placed(parts[1], gx + 1)]
+        for side in (4, 5, 2, 3):
+            tiles.append(placed(parts[side], gx))
+        joined = zero
+        for k, dot in enumerate(dots):
+            dot = dot + pltpu.roll(dot, 64, 1)
+            joined = jnp.where(lane8 >> 5 == k, dot + pltpu.roll(dot, 32, 1), joined)
+        return rows_of(tiles + [joined, zero, zero])[:6]
 
     def neighbour_parts(e):
         parts = [
@@ -440,31 +435,26 @@
         pltpu.make_async_copy(part, part, gr_sem.at[g, ph]).wait()
         pltpu.make_async_copy(part, part, gs_sem.at[g, ph]).wait()
 
-    def group_lines(slots):
-        return [transpose_groups(slots[nx * c : nx * (c + 1)]) for c in range(2)]
-
-    def gather(g, line, started, between):
-        G1[g - 1, pl.ds(phases[0][0], 1), :] = line
+    def gather(g, tile, started, between):
+        G1[g - 1, phases[0][0]] = tile
         phase_start(g, 0)
         started()
         phase_wait(g, 0)
-        tiles = group_lines(G1.at[g - 1])
-
-        def pick(group):
-            return jnp.concatenate([tile[group : group + 1] for tile in tiles], axis=0)
-
-        lane2 = lax.broadcasted_iota(jnp.int32, (2, 128), 1)
-        own = pick(0)
-        own = own + jnp.where(lane2 < 112, pltpu.roll(pick(1), 112, 1), 0.0)
-        own = own + jnp.where(lane2 >= 16, pltpu.roll(pick(2), 16, 1), 0.0)
-        own = own + jnp.concatenate([tiles[1][5:6], tiles[0][6:7]], axis=0)
+        low, high = [jnp.sum(G1[g - 1, nx * c : nx * (c + 1)], axis=0) for c in range(2)]
         slot = phases[1][0]
-        G2[g - 1, slot, 0:2] = own
-        G2[g - 1, slot, 2:4] = pick(3)
-        G2[g - 1, slot, 4:6] = pick(4)
-        G2[g - 1, slot, 6:7] = tiles[0][5:6]
-        G2[g - 1, slot, 7:8] = tiles[1][6:7]
-        G2[g - 1, slot, 8:9] = tiles[0][7:8] + tiles[1][7:8]
+        rows = [
+            low[0:1] + high[3:4],
+            high[0:1] + low[4:5],
+            low[1:2],
+            high[1:2],
+            low[2:3],
+            high[2:3],
+            low[3:4],
+            high[4:5],
+            low[5:6] + high[5:6],
+        ]
+        for k, row in enumerate(rows):
+            G2[g - 1, slot, k : k + 1] = row
         phase_start(g, 1)
         between()
         phase_wait(g, 1)
@@ -474,31 +464,33 @@
         lane = lax.broadcasted_iota(jnp.int32, (1, 128), 1)
         return [
             jnp.broadcast_to(
-                jnp.sum(jnp.where(lane & 15 == k, row, 0.0), axis=1, keepdims=True), (1, 128)
+                jnp.sum(jnp.where(lane >> 5 == k, row, 0.0), axis=1, keepdims=True), (1, 128)
             )
             for k in range(3)
         ]
 
     def right_side(g):
+        def row(slot, k):
+            if isinstance(g, int):
+                return jnp.broadcast_to(G2_first[slot, k : k + 1], (8, 128))
+            return jnp.broadcast_to(G2[g - 1, slot, k : k + 1], (8, 128))
+
         rows = [[None] * ny for _ in range(nz)]
         for j in range(ny):
             for k in range(chips):
                 slot = j * chips + k
-                if isinstance(g, int):
-                    pairs = G2_first[slot]
-                    low, high = pairs[0:1], pairs[1:2]
-                else:
-                    pairs = G2[g - 1, slot, 0:2]
-                    if j + 1 < ny:
-                        pairs = pairs + G2[g - 1, slot + chips, 2:4]
-                    if j > 0:
-                        pairs = pairs + G2[g - 1, slot - chips, 4:6]
-                    low, high = pairs[0:1], pairs[1:2]
-                    if k > 0:
-                        low = low + G2[g - 1, slot - 1, 7:8]
-                    if k + 1 < chips:
-                        high = high + G2[g - 1, slot + 1, 6:7]
-                rows[2 * k][j], rows[2 * k + 1][j] = low, high
+                for c in range(2):
+                    total = row(slot, c)
+                    if not isinstance(g, int):
+                        if j + 1 < ny:
+                            total = total + row(slot + chips, 2 + c)
+                        if j > 0:
+                            total = total + row(slot - chips, 4 + c)
+                        if c == 0 and k > 0:
+                            total = total + row(slot - 1, 7)
+                        if c == 1 and k + 1 < chips:
+                            total = total + row(slot + 1, 6)
+                    rows[2 * k + c][j] = total
         return rows
 
     def coarse(g):
@@ -506,7 +498,7 @@
         for i, rows in enumerate(right_side(g)):
             for j in range(ny):
                 columns = slice((i * ny + j) * 128, (i * ny + j + 1) * 128)
-                row = rows[j]
+                row = jnp.concatenate([rows[j], rows[j]], axis=0)
                 accs[6] = accs[6] + inv[:, columns] * row
                 for side in range(6):
                     accs[side] = accs[side] + inv_far[side, :, columns] * row
@@ -548,15 +540,6 @@
             ey[low] = fyb[low] * (y_own[low] - y_far[low])
         for half in range(2):
             spread(fzp[half] * (z_own[half] - z_far[half]), half)
-
-    loads[0].wait()
-    loads[1].wait()
-    sums = lax.fori_loop(0, cx, restrict_rhs, no_sums, unroll=4)
-    line = message([label_sums(sums)], ())
-    pl.semaphore_wait(barrier, len(partners))
-    G1_first[pl.ds(phases[0][0], 1), :] = line
-    phase_start(0, 0)
-    loads[2].wait()
 
     def order_columns():
         for top in (0, 8):
@@ -572,6 +555,17 @@
                 for i in range(nz):
                     inv[top : top + 8, pl.ds((i * ny + j) * 128, 128)] = tiles[i]
 
+    loads[0].wait()
+    loads[1].wait()
+    sums = lax.fori_loop(0, cx, restrict_rhs, no_sums, unroll=4)
+    line = jnp.sum(placed(label_sums(sums), gx), axis=0, keepdims=True)
+    loads[3].wait()
+    order_columns()
+    pl.semaphore_wait(barrier, len(partners))
+    G1_first[pl.ds(phases[0][0], 1), :] = line
+    phase_start(0, 0)
+    loads[2].wait()
+
     def stage_static(x, carry):
         mobility = interleaved(mob_in, x)
         mob[x + 1] = mobility
@@ -587,8 +581,6 @@
         lzs[half] = pack_end(lt, half)
     exchange_start(MOB)
     exchange_start(LAB)
-    loads[3].wait()
-    order_columns()
     exchange_start(INV)
 
     def faces():
@@ -630,7 +622,7 @@
 
     phase_wait(0, 0)
     G2_first[phases[1][0]] = jnp.concatenate(
-        [tile[0:1] for tile in group_lines(G1_first)], axis=0
+        [jnp.sum(G1_first[nx * c : nx * (c + 1)], axis=0, keepdims=True) for c in range(2)], axis=0
     )
     phase_start(0, 1)
     faces()
@@ -669,7 +661,7 @@
         sums, parts = coarse_right_side(k)
         gather(
             k + 1,
-            message([sums] + [parts[side] for side in (0, 1, 4, 5, 2, 3)], dots),
+            message(sums, parts, dots),
             lambda: exchange_start(k),
             lambda: exchange_wait(k),
         )
@@ -815,7 +807,7 @@
                 vmem(2, cx, cz),
                 vmem(2 * nx, 128),
                 vmem(ny * nz // 2, 2, 128),
-                vmem(STEPS, 2 * nx, 128),
+                vmem(STEPS, 2 * nx, 6, 128),
                 vmem(STEPS, ny * nz // 2, 9, 128),
                 vmem(2 * nx, 128),
                 vmem(ny * nz // 2, 128),

time: 74.2 us -> 73.4 us (0.989)
  Pallas kernels: 70.7 us -> 69.9 us
    pallas_call x1, Pallas kernels: 70.7 us -> 69.9 us  [per_device(): pl.pallas_call(functools.partial(kernel, nx, ny, nz), out_shape=[jax.Shap...]
where the time goes in v6:
time: 73.4 us; the launch traced here: 73.3 us
  Pallas kernels  69.9 us (95%)
  other arithmetic  2.72 us (4%)
    pallas_call x1, Pallas kernels, per_device(): pl.pallas_call(functools.partial(kernel, nx, ny, nz), out_shape=[jax.Shap...  69.9 us
    sub x1, other arithmetic, per_device(): return (xs + alpha * p, rs - alpha * w)  2.72 us

profile of v6, /device:TPU:1, one launch (start us, length us, event | category | flops | bytes accessed | tf_op | source)
XLA Modules:
  0.0 73.3 jit_solution(2270429709867296765)
XLA Ops:
  0.6 69.9 %deflated_cg.1 = (f32[16,64,128]{2,1,0:T(8,128)}, f32[16,64,128]{2,1,0:T(8,128)}, f32[16,64,128]{2,1,0:T(8,128)}, f32[16,64,128]{2,1,0:T(8,128)}, f32[64,128]{1,0:T(8,128)}) custom-call(f32[16,64,128]{2,1,0:T(8,128)} %rhs_hbm.1, f32[16,64,128]{2,1,0:T(8,128)} %mob_hbm.1, s32[16,64,128]{2,1,0:T(8,128)} %lab_hbm.1, f32[16,4096]{1,0:T(8,128)} %inv_hbm.1), custom_call_target="tpu_custom_call" | custom-call | tf_op jit(solution)/shard_map/deflated_cg/pallas_call | solution.py:764
  70.6 2.7 %multiply_subtract_fusion = (f32[16,64,128]{2,1,0:T(8,128)}, f32[16,64,128]{2,1,0:T(8,128)}) fusion(f32[16,64,128]{2,1,0:T(8,128)} %get-tuple-element.10, f32[16,64,128]{2,1,0:T(8,128)} %get-tuple-element.11, f32[64,128]{1,0:T(8,128)} %get-tuple-element.8, f32[16,64,128]{2,1,0:T(8,128)} %get-tuple-element.7, f32[16,64,128]{2,1,0:T(8,128)} %get-tuple-element.9), kind=kLoop, calls=%fused_computation | loop fusion | flops 524288 | bytes 3178496 | tf_op jit(solution)/shard_map/sub | solution.py:826

commit v7 on v6

--- a/solution.py
+++ b/solution.py
@@ -113,30 +113,6 @@
     for load in loads:
         load.start()
 
-    def clear(ref, *index):
-        ref[index or Ellipsis] = jnp.zeros(ref.shape[len(index) :], ref.dtype)
-
-    for low in range(2):
-
-        @pl.when(gx == (nx - 1 if low else 0))
-        def _():
-            clear(mob, cx + 1 if low else 0)
-            clear(lxh, low)
-            for e in range(STEPS):
-                clear(xh, e, low)
-
-        @pl.when(gz == (nz - 1 if low else 0))
-        def _():
-            clear(lyh, low)
-            for e in range(STEPS + 1):
-                clear(yh, e, low)
-
-        @pl.when(gy == (ny - 1 if low else 0))
-        def _():
-            clear(lzh, low)
-            for e in range(STEPS + 1):
-                clear(zh, e, low)
-
     barrier = pltpu.get_barrier_semaphore()
     chips = nz // 2
     chip, core = lax.div(gz, 2), lax.rem(gz, 2)
@@ -156,6 +132,30 @@
     partners = line_peers + plane_peers + [logical(gx, gy, gz + nz - 1 + 2 * core)]
     for partner in partners:
         pl.semaphore_signal(barrier, inc=1, device_id=partner, device_id_type=LOGICAL)
+
+    def clear(ref, *index):
+        ref[index or Ellipsis] = jnp.zeros(ref.shape[len(index) :], ref.dtype)
+
+    for low in range(2):
+
+        @pl.when(gx == (nx - 1 if low else 0))
+        def _():
+            clear(mob, cx + 1 if low else 0)
+            clear(lxh, low)
+            for e in range(STEPS):
+                clear(xh, e, low)
+
+        @pl.when(gz == (nz - 1 if low else 0))
+        def _():
+            clear(lyh, low)
+            for e in range(STEPS + 1):
+                clear(yh, e, low)
+
+        @pl.when(gy == (ny - 1 if low else 0))
+        def _():
+            clear(lzh, low)
+            for e in range(STEPS + 1):
+                clear(zh, e, low)
 
     clear(field, 0)
     clear(field, cx + 1)
@@ -555,17 +555,6 @@
                 for i in range(nz):
                     inv[top : top + 8, pl.ds((i * ny + j) * 128, 128)] = tiles[i]
 
-    loads[0].wait()
-    loads[1].wait()
-    sums = lax.fori_loop(0, cx, restrict_rhs, no_sums, unroll=4)
-    line = jnp.sum(placed(label_sums(sums), gx), axis=0, keepdims=True)
-    loads[3].wait()
-    order_columns()
-    pl.semaphore_wait(barrier, len(partners))
-    G1_first[pl.ds(phases[0][0], 1), :] = line
-    phase_start(0, 0)
-    loads[2].wait()
-
     def stage_static(x, carry):
         mobility = interleaved(mob_in, x)
         mob[x + 1] = mobility
@@ -575,10 +564,20 @@
         lt[x] = pack_plane(labels)
         return carry
 
+    loads[0].wait()
+    loads[1].wait()
+    sums = lax.fori_loop(0, cx, restrict_rhs, no_sums, unroll=4)
+    line = jnp.sum(placed(label_sums(sums), gx), axis=0, keepdims=True)
+    loads[3].wait()
+    order_columns()
+    loads[2].wait()
     lax.fori_loop(0, cx, stage_static, 0, unroll=4)
     stage_end(MOB)
     for half in range(2):
         lzs[half] = pack_end(lt, half)
+    pl.semaphore_wait(barrier, len(partners))
+    G1_first[pl.ds(phases[0][0], 1), :] = line
+    phase_start(0, 0)
     exchange_start(MOB)
     exchange_start(LAB)
     exchange_start(INV)

time: 73.4 us -> 72.8 us (level)
  no operation moved by 1% of the time
where the time goes in v7:
time: 72.8 us; the launch traced here: 72.7 us
  Pallas kernels  69.3 us (95%)
  other arithmetic  2.72 us (4%)
    pallas_call x1, Pallas kernels, per_device(): pl.pallas_call(functools.partial(kernel, nx, ny, nz), out_shape=[jax.Shap...  69.3 us
    sub x1, other arithmetic, per_device(): return (xs + alpha * p, rs - alpha * w)  2.72 us

profile of v7, /device:TPU:1, one launch (start us, length us, event | category | flops | bytes accessed | tf_op | source)
XLA Modules:
  0.0 72.7 jit_solution(10983002157882366)
XLA Ops:
  0.6 69.3 %deflated_cg.1 = (f32[16,64,128]{2,1,0:T(8,128)}, f32[16,64,128]{2,1,0:T(8,128)}, f32[16,64,128]{2,1,0:T(8,128)}, f32[16,64,128]{2,1,0:T(8,128)}, f32[64,128]{1,0:T(8,128)}) custom-call(f32[16,64,128]{2,1,0:T(8,128)} %rhs_hbm.1, f32[16,64,128]{2,1,0:T(8,128)} %mob_hbm.1, s32[16,64,128]{2,1,0:T(8,128)} %lab_hbm.1, f32[16,4096]{1,0:T(8,128)} %inv_hbm.1), custom_call_target="tpu_custom_call" | custom-call | tf_op jit(solution)/shard_map/deflated_cg/pallas_call | solution.py:763
  70.0 2.7 %multiply_subtract_fusion = (f32[16,64,128]{2,1,0:T(8,128)}, f32[16,64,128]{2,1,0:T(8,128)}) fusion(f32[16,64,128]{2,1,0:T(8,128)} %get-tuple-element.10, f32[16,64,128]{2,1,0:T(8,128)} %get-tuple-element.11, f32[64,128]{1,0:T(8,128)} %get-tuple-element.8, f32[16,64,128]{2,1,0:T(8,128)} %get-tuple-element.7, f32[16,64,128]{2,1,0:T(8,128)} %get-tuple-element.9), kind=kLoop, calls=%fused_computation | loop fusion | flops 524288 | bytes 3178496 | tf_op jit(solution)/shard_map/sub | solution.py:825

commit v8 on v7

--- a/solution.py
+++ b/solution.py
@@ -319,11 +319,11 @@
         )
         return step(cx - 1, carry, values[cx + 1])[2]
 
-    def subset_sums(values, bits):
-        terms = [values]
-        for bit in bits:
+    def add_tile(sums, tile, tile_bits):
+        terms = [tile]
+        for bit in tile_bits:
             terms = terms + [term * bit for term in terms]
-        return [fold(term) for term in terms]
+        return [total + term for total, term in zip(sums, terms)]
 
     def label_sums(sums):
         sums = list(sums)
@@ -337,21 +337,29 @@
         return [((labels >> i) & 1).astype(F32) for i in range(4)]
 
     def by_label(labels, values):
-        return label_sums(subset_sums(values, bits_of(labels)))
+        sums = no_sums
+        for k in range(0, values.shape[0], 8):
+            sums = add_tile(sums, values[k : k + 8], bits_of(labels[k : k + 8]))
+        return label_sums(sums)
 
     def restrict_plane(x, plane, sums):
-        more = subset_sums(plane, [bits[i, x] for i in range(4)])
-        return tuple(total + extra for total, extra in zip(sums, more))
+        for k in range(0, 64, 8):
+            tile_bits = [bits[i, x, k : k + 8] for i in range(4)]
+            sums = add_tile(sums, plane[k : k + 8], tile_bits)
+        return tuple(sums)
 
     def restrict_rhs(x, sums):
-        labels = interleaved(lab_in, x)
-        values = interleaved(rhs_in, x)
-        lab[x] = labels
-        rhs[x] = values
-        planes = bits_of(labels)
-        for i in range(4):
-            bits[i, x] = planes[i]
-        return tuple(total + extra for total, extra in zip(sums, subset_sums(values, planes)))
+        for k in range(8):
+            labels = lab_in[x, pl.ds(k, 8, stride=8), :]
+            values = rhs_in[x, pl.ds(k, 8, stride=8), :]
+            tile_bits = bits_of(labels)
+            rows = slice(8 * k, 8 * k + 8)
+            lab[x, rows] = labels
+            rhs[x, rows] = values
+            for i in range(4):
+                bits[i, x, rows] = tile_bits[i]
+            sums = add_tile(sums, values, tile_bits)
+        return tuple(sums)
 
     no_sums = (zero,) * 16
 
@@ -512,27 +520,42 @@
             values.append(total)
         return values
 
-    def take(values, masks):
-        picked = [jnp.broadcast_to(values[m : m + 1], masks[0].shape) for m in range(16)]
-        for mask in masks:
-            picked = [jnp.where(mask, b, a) for a, b in zip(picked[::2], picked[1::2])]
-        return picked[0]
+    def splats_of(values):
+        return [jnp.broadcast_to(values[m : m + 1], (8, 128)) for m in range(16)]
+
+    def pick(splats, masks):
+        if len(splats) == 1:
+            return splats[0]
+        half = len(splats) // 2
+        return jnp.where(
+            masks[-1], pick(splats[half:], masks[:-1]), pick(splats[:half], masks[:-1])
+        )
 
     def masks_of(labels):
         return [labels & (1 << i) != 0 for i in range(4)]
 
-    def take_plane(values, x):
-        return take(values, [bits[i, x] > 0.5 for i in range(4)])
+    def take(splats, labels):
+        tiles = [
+            pick(splats, masks_of(labels[k : k + 8])) for k in range(0, labels.shape[0], 8)
+        ]
+        return jnp.concatenate(tiles, axis=0)
+
+    def take_plane(splats, x):
+        tiles = [
+            pick(splats, [bits[i, x, k : k + 8] > 0.5 for i in range(4)]) for k in range(0, 64, 8)
+        ]
+        return jnp.concatenate(tiles, axis=0)
 
     def rim_of(values):
-        x_far = [take(values[low], masks_of(lxh[low])) for low in range(2)]
-        y_own = [take(values[6], masks_of(lys[low])) for low in range(2)]
-        y_far = [take(values[2 + low], masks_of(lyh[low])) for low in range(2)]
-        z_own = [take(values[6], masks_of(lzs[half])) for half in range(2)]
-        z_far = []
-        for half in range(2):
-            masks = masks_of(lzf[half])
-            z_far.append(jnp.where(even, take(values[4], masks), take(values[5], masks)))
+        splats = [splats_of(value) for value in values]
+        x_far = [take(splats[low], lxh[low]) for low in range(2)]
+        y_own = [take(splats[6], lys[low]) for low in range(2)]
+        y_far = [take(splats[2 + low], lyh[low]) for low in range(2)]
+        z_own = [take(splats[6], lzs[half]) for half in range(2)]
+        z_far = [
+            jnp.where(even, take(splats[4], lzf[half]), take(splats[5], lzf[half]))
+            for half in range(2)
+        ]
         return x_far, y_own, y_far, z_own, z_far
 
     def outer_faces(y_own, y_far, z_own, z_far):
@@ -630,8 +653,10 @@
     exchange_wait(INV)
     lines = coarse(0)
 
+    own_splats = splats_of(lines[6])
+
     def first_iterate(x):
-        plane = take_plane(lines[6], x)
+        plane = take_plane(own_splats, x)
         x0[x + 1] = plane
         return plane
 
@@ -695,10 +720,12 @@
             [prim_z[2], prim_z[3]],
         )
 
+        splats = splats_of(lines[6])
+
         def next_direction(x):
             residual = rs[x] - alpha * ws[x]
             rs[x] = residual
-            plane = (residual * dinv[x] + beta * direction[x + 1]) - take_plane(lines[6], x)
+            plane = (residual * dinv[x] + beta * direction[x + 1]) - take_plane(splats, x)
             direction[x + 1] = plane
             history[k, x] = plane
             return plane

time: 72.8 us -> 72.7 us (level)
  no operation moved by 1% of the time
where the time goes in v8:
time: 72.7 us; the launch traced here: 72.6 us
  Pallas kernels  69.2 us (95%)
  other arithmetic  2.72 us (4%)
    pallas_call x1, Pallas kernels, per_device(): pl.pallas_call(functools.partial(kernel, nx, ny, nz), out_shape=[jax.Shap...  69.2 us
    sub x1, other arithmetic, per_device(): return (xs + alpha * p, rs - alpha * w)  2.72 us

profile of v8, /device:TPU:1, one launch (start us, length us, event | category | flops | bytes accessed | tf_op | source)
XLA Modules:
  0.0 72.6 jit_solution(15003141401494555220)
XLA Ops:
  0.6 69.2 %deflated_cg.1 = (f32[16,64,128]{2,1,0:T(8,128)}, f32[16,64,128]{2,1,0:T(8,128)}, f32[16,64,128]{2,1,0:T(8,128)}, f32[16,64,128]{2,1,0:T(8,128)}, f32[64,128]{1,0:T(8,128)}) custom-call(f32[16,64,128]{2,1,0:T(8,128)} %rhs_hbm.1, f32[16,64,128]{2,1,0:T(8,128)} %mob_hbm.1, s32[16,64,128]{2,1,0:T(8,128)} %lab_hbm.1, f32[16,4096]{1,0:T(8,128)} %inv_hbm.1), custom_call_target="tpu_custom_call" | custom-call | tf_op jit(solution)/shard_map/deflated_cg/pallas_call | solution.py:790
  69.9 2.7 %multiply_subtract_fusion = (f32[16,64,128]{2,1,0:T(8,128)}, f32[16,64,128]{2,1,0:T(8,128)}) fusion(f32[16,64,128]{2,1,0:T(8,128)} %get-tuple-element.10, f32[16,64,128]{2,1,0:T(8,128)} %get-tuple-element.11, f32[64,128]{1,0:T(8,128)} %get-tuple-element.8, f32[16,64,128]{2,1,0:T(8,128)} %get-tuple-element.7, f32[16,64,128]{2,1,0:T(8,128)} %get-tuple-element.9), kind=kLoop, calls=%fused_computation | loop fusion | flops 524288 | bytes 3178496 | tf_op jit(solution)/shard_map/sub | solution.py:852

commit v9 on v8

--- a/solution.py
+++ b/solution.py
@@ -279,33 +279,46 @@
         for k in range(1, 8):
             et[8 * half + k] = pltpu.roll(packed, 128 - 16 * k, 1)
 
-    def edge_part(x, v):
-        return edge_tiles(x)
+    def edge_tile(x, k):
+        tile = et[x]
+        tile = jnp.where(ends, pltpu.roll(tile, 128 - 2 * k, 1) if k else tile, 0.0)
+        if k == 0:
+            tile = tile + jnp.where(row8 == 0, ey[0, pl.ds(x, 1), :], 0.0)
+        if k == 7:
+            tile = tile + jnp.where(row8 == 7, ey[1, pl.ds(x, 1), :], 0.0)
+        return tile
+
+    def edge_part(x, k, v):
+        return edge_tile(x, k)
 
     def edge_tiles(x):
-        tile = et[x]
-        tiles = [
-            jnp.where(ends, tile if k == 0 else pltpu.roll(tile, 128 - 2 * k, 1), 0.0)
-            for k in range(8)
-        ]
-        first, last = ey[0, pl.ds(x, 1), :], ey[1, pl.ds(x, 1), :]
-        tiles[0] = tiles[0] + jnp.where(row8 == 0, first, 0.0)
-        tiles[7] = tiles[7] + jnp.where(row8 == 7, last, 0.0)
-        return jnp.concatenate(tiles, axis=0)
-
-    def apply_all(values, body, init, outer, make=None):
+        return jnp.concatenate([edge_tile(x, k) for k in range(8)], axis=0)
+
+    def apply_all(values, body, init, outer, make=None, stage=None):
         def step(x, carry, above_v):
             below, v, rest = carry
-            above = fx[x + 1] * (above_v - v)
-            flux_y = fy[x] * (next_row(v) - v)
-            flux_z = fz[x] * (pltpu.roll(v, 127, 1) - v)
-            out = (
-                (below - above)
-                + (last_row(flux_y) - flux_y)
-                + (pltpu.roll(flux_z, 1, 1) - flux_z)
-                + outer(x, v)
-            )
-            return above, above_v, body(x, v, out, rest)
+            tiles = [v[8 * k : 8 * k + 8] for k in range(8)]
+            last = fy[x, 56:64] * (pltpu.roll(tiles[0], 7, 0) - tiles[7])
+            flux_below = pltpu.roll(last, 1, 0)
+            aboves = []
+            for k in range(8):
+                rows = slice(8 * k, 8 * k + 8)
+                tile = tiles[k]
+                above = fx[x + 1, rows] * (above_v[rows] - tile)
+                flux_y = fy[x, rows] * (tiles[k + 1] - tile) if k < 7 else last
+                flux_z = fz[x, rows] * (pltpu.roll(tile, 127, 1) - tile)
+                out = (
+                    (below[rows] - above)
+                    + (flux_below - flux_y)
+                    + (pltpu.roll(flux_z, 1, 1) - flux_z)
+                    + outer(x, k, tile)
+                )
+                flux_below = flux_y
+                aboves.append(above)
+                rest = body(x, k, tile, out, rest)
+            if stage is not None:
+                stage_plane(stage, x, field[x + 1])
+            return jnp.concatenate(aboves, axis=0), above_v, rest
 
         if make is None:
 
@@ -342,11 +355,9 @@
             sums = add_tile(sums, values[k : k + 8], bits_of(labels[k : k + 8]))
         return label_sums(sums)
 
-    def restrict_plane(x, plane, sums):
-        for k in range(0, 64, 8):
-            tile_bits = [bits[i, x, k : k + 8] for i in range(4)]
-            sums = add_tile(sums, plane[k : k + 8], tile_bits)
-        return tuple(sums)
+    def restrict_tile(x, k, tile, sums):
+        rows = slice(8 * k, 8 * k + 8)
+        return tuple(add_tile(sums, tile, [bits[i, x, rows] for i in range(4)]))
 
     def restrict_rhs(x, sums):
         for k in range(8):
@@ -412,7 +423,10 @@
 
     def coarse_right_side(e):
         sums = apply_all(
-            field, lambda x, v, out, s: restrict_plane(x, out, s), no_sums, lambda x, v: rim[x] * v
+            field,
+            lambda x, k, v, out, s: restrict_tile(x, k, out, s),
+            no_sums,
+            lambda x, k, v: rim[x, 8 * k : 8 * k + 8] * v,
         )
         return label_sums(sums), neighbour_parts(e)
 
@@ -665,15 +679,15 @@
     x0[cx + 1] = x_far[1]
     outer_faces(*rest)
 
-    def first_residual(x, v, out, dot):
-        residual = rhs[x] - out
-        precond = residual * dinv[x]
-        rs[x] = residual
-        field[x + 1] = precond
-        stage_plane(0, x, precond)
-        return dot + fold(residual * precond)
-
-    ry_part = apply_all(x0, first_residual, zero, edge_part, first_iterate)
+    def first_residual(x, k, v, out, dot):
+        rows = slice(8 * k, 8 * k + 8)
+        residual = rhs[x, rows] - out
+        precond = residual * dinv[x, rows]
+        rs[x, rows] = residual
+        field[x + 1, rows] = precond
+        return dot + residual * precond
+
+    ry_part = apply_all(x0, first_residual, zero, edge_part, first_iterate, 0)
     stage_end(0)
 
     def tall(row):
@@ -730,18 +744,14 @@
             history[k, x] = plane
             return plane
 
-        def image(x, v, out, dots):
-            z = out * dinv[x]
-            ws[x] = out
-            field[x + 1] = z
-            stage_plane(k + 1, x, z)
-            return (
-                dots[0] + fold(v * out),
-                dots[1] + fold(rs[x] * z),
-                dots[2] + fold(out * z),
-            )
-
-        dots = apply_all(direction, image, (zero, zero, zero), edge_part, next_direction)
+        def image(x, i, v, out, dots):
+            rows = slice(8 * i, 8 * i + 8)
+            z = out * dinv[x, rows]
+            ws[x, rows] = out
+            field[x + 1, rows] = z
+            return dots[0] + v * out, dots[1] + rs[x, rows] * z, dots[2] + out * z
+
+        dots = apply_all(direction, image, (zero, zero, zero), edge_part, next_direction, k + 1)
         stage_end(k + 1)
         return tall(ry_next), lines, dots, last_alpha, tall(alpha)
 

time: 72.7 us -> 72.7 us (level)
  no operation moved by 1% of the time
where the time goes in v9:
time: 72.7 us; the launch traced here: 72.6 us
  Pallas kernels  69.2 us (95%)
  other arithmetic  2.72 us (4%)
    pallas_call x1, Pallas kernels, per_device(): pl.pallas_call(functools.partial(kernel, nx, ny, nz), out_shape=[jax.Shap...  69.2 us
    sub x1, other arithmetic, per_device(): return (xs + alpha * p, rs - alpha * w)  2.72 us

profile of v9, /device:TPU:1, one launch (start us, length us, event | category | flops | bytes accessed | tf_op | source)
XLA Modules:
  0.0 72.6 jit_solution(7122296984076374997)
XLA Ops:
  0.6 69.2 %deflated_cg.1 = (f32[16,64,128]{2,1,0:T(8,128)}, f32[16,64,128]{2,1,0:T(8,128)}, f32[16,64,128]{2,1,0:T(8,128)}, f32[16,64,128]{2,1,0:T(8,128)}, f32[64,128]{1,0:T(8,128)}) custom-call(f32[16,64,128]{2,1,0:T(8,128)} %rhs_hbm.1, f32[16,64,128]{2,1,0:T(8,128)} %mob_hbm.1, s32[16,64,128]{2,1,0:T(8,128)} %lab_hbm.1, f32[16,4096]{1,0:T(8,128)} %inv_hbm.1), custom_call_target="tpu_custom_call" | custom-call | tf_op jit(solution)/shard_map/deflated_cg/pallas_call | solution.py:800
  69.9 2.7 %multiply_subtract_fusion = (f32[16,64,128]{2,1,0:T(8,128)}, f32[16,64,128]{2,1,0:T(8,128)}) fusion(f32[16,64,128]{2,1,0:T(8,128)} %get-tuple-element.10, f32[16,64,128]{2,1,0:T(8,128)} %get-tuple-element.11, f32[64,128]{1,0:T(8,128)} %get-tuple-element.8, f32[16,64,128]{2,1,0:T(8,128)} %get-tuple-element.7, f32[16,64,128]{2,1,0:T(8,128)} %get-tuple-element.9), kind=kLoop, calls=%fused_computation | loop fusion | flops 524288 | bytes 3178496 | tf_op jit(solution)/shard_map/sub | solution.py:862

commit v10 on v9

--- a/solution.py
+++ b/solution.py
@@ -9,7 +9,7 @@
 
 LOGICAL = pl.DeviceIdType.LOGICAL
 F32 = jnp.float32
-LOOP = 5
+LOOP = 3
 VMEM_BYTES = 64 * 1024 * 1024 - 256 * 1024
 
 STEPS = 3
@@ -620,12 +620,8 @@
     exchange_start(INV)
 
     def faces():
-        for ref in (direction, ws, yrim_x, yrim_y, yrim_z, prim_y, prim_z):
-            clear(ref)
         exchange_wait(MOB)
-        exchange_wait(LAB)
         for half in range(2):
-            lzf[half] = far(lzh, half)
             fzp[half] = 0.5 * (zs[MOB, half] + far(zh.at[MOB], half))
             spread(fzp[half], half)
         for low in range(2):
@@ -655,7 +651,12 @@
             return above
 
         lax.fori_loop(0, cx, step, fx[0], unroll=4)
-
+        exchange_wait(LAB)
+        for half in range(2):
+            lzf[half] = far(lzh, half)
+
+    for ref in (direction, ws, yrim_x, yrim_y, yrim_z, prim_y, prim_z):
+        clear(ref)
     phase_wait(0, 0)
     G2_first[phases[1][0]] = jnp.concatenate(
         [jnp.sum(G1_first[nx * c : nx * (c + 1)], axis=0, keepdims=True) for c in range(2)], axis=0

time: 72.7 us -> 75.1 us (1.033)
  Pallas kernels: 69.2 us -> 71.6 us
    pallas_call x1, Pallas kernels: 69.2 us -> 71.6 us  [per_device(): pl.pallas_call(functools.partial(kernel, nx, ny, nz), out_shape=[jax.Shap...]
where the time goes in v10:
time: 75.1 us; the launch traced here: 74.9 us
  Pallas kernels  71.6 us (95%)
  other arithmetic  2.72 us (4%)
    pallas_call x1, Pallas kernels, per_device(): pl.pallas_call(functools.partial(kernel, nx, ny, nz), out_shape=[jax.Shap...  71.6 us
    sub x1, other arithmetic, per_device(): return (xs + alpha * p, rs - alpha * w)  2.72 us

profile of v10, /device:TPU:1, one launch (start us, length us, event | category | flops | bytes accessed | tf_op | source)
XLA Modules:
  0.0 74.9 jit_solution(2996625422642273863)
XLA Ops:
  0.6 71.6 %deflated_cg.1 = (f32[16,64,128]{2,1,0:T(8,128)}, f32[16,64,128]{2,1,0:T(8,128)}, f32[16,64,128]{2,1,0:T(8,128)}, f32[16,64,128]{2,1,0:T(8,128)}, f32[64,128]{1,0:T(8,128)}) custom-call(f32[16,64,128]{2,1,0:T(8,128)} %rhs_hbm.1, f32[16,64,128]{2,1,0:T(8,128)} %mob_hbm.1, s32[16,64,128]{2,1,0:T(8,128)} %lab_hbm.1, f32[16,4096]{1,0:T(8,128)} %inv_hbm.1), custom_call_target="tpu_custom_call" | custom-call | tf_op jit(solution)/shard_map/deflated_cg/pallas_call | solution.py:801
  72.2 2.7 %multiply_subtract_fusion = (f32[16,64,128]{2,1,0:T(8,128)}, f32[16,64,128]{2,1,0:T(8,128)}) fusion(f32[16,64,128]{2,1,0:T(8,128)} %get-tuple-element.10, f32[16,64,128]{2,1,0:T(8,128)} %get-tuple-element.11, f32[64,128]{1,0:T(8,128)} %get-tuple-element.8, f32[16,64,128]{2,1,0:T(8,128)} %get-tuple-element.7, f32[16,64,128]{2,1,0:T(8,128)} %get-tuple-element.9), kind=kLoop, calls=%fused_computation | loop fusion | flops 524288 | bytes 3178496 | tf_op jit(solution)/shard_map/sub | solution.py:863

commit v11 on v8

--- a/solution.py
+++ b/solution.py
@@ -9,7 +9,7 @@
 
 LOGICAL = pl.DeviceIdType.LOGICAL
 F32 = jnp.float32
-LOOP = 5
+LOOP = 15
 VMEM_BYTES = 64 * 1024 * 1024 - 256 * 1024
 
 STEPS = 3

time: 72.7 us -> 72.4 us (level)
  no operation moved by 1% of the time
where the time goes in v11:
time: 72.4 us; the launch traced here: 72.2 us
  Pallas kernels  68.9 us (95%)
  other arithmetic  2.72 us (4%)
    pallas_call x1, Pallas kernels, per_device(): pl.pallas_call(functools.partial(kernel, nx, ny, nz), out_shape=[jax.Shap...  68.9 us
    sub x1, other arithmetic, per_device(): return (xs + alpha * p, rs - alpha * w)  2.72 us

profile of v11, /device:TPU:1, one launch (start us, length us, event | category | flops | bytes accessed | tf_op | source)
XLA Modules:
  0.0 72.2 jit_solution(16613297003335326055)
XLA Ops:
  0.6 68.9 %deflated_cg.1 = (f32[16,64,128]{2,1,0:T(8,128)}, f32[16,64,128]{2,1,0:T(8,128)}, f32[16,64,128]{2,1,0:T(8,128)}, f32[16,64,128]{2,1,0:T(8,128)}, f32[64,128]{1,0:T(8,128)}) custom-call(f32[16,64,128]{2,1,0:T(8,128)} %rhs_hbm.1, f32[16,64,128]{2,1,0:T(8,128)} %mob_hbm.1, s32[16,64,128]{2,1,0:T(8,128)} %lab_hbm.1, f32[16,4096]{1,0:T(8,128)} %inv_hbm.1), custom_call_target="tpu_custom_call" | custom-call | tf_op jit(solution)/shard_map/deflated_cg/pallas_call | solution.py:790
  69.5 2.7 %multiply_subtract_fusion = (f32[16,64,128]{2,1,0:T(8,128)}, f32[16,64,128]{2,1,0:T(8,128)}) fusion(f32[16,64,128]{2,1,0:T(8,128)} %get-tuple-element.10, f32[16,64,128]{2,1,0:T(8,128)} %get-tuple-element.11, f32[64,128]{1,0:T(8,128)} %get-tuple-element.8, f32[16,64,128]{2,1,0:T(8,128)} %get-tuple-element.7, f32[16,64,128]{2,1,0:T(8,128)} %get-tuple-element.9), kind=kLoop, calls=%fused_computation | loop fusion | flops 524288 | bytes 3178496 | tf_op jit(solution)/shard_map/sub | solution.py:852
